TPU v7x, 128 devices: a whole 4x4x4 slice. The times are simulated.
128 devices in a mesh: ckpt: 4 (over z_lo, core), wide: 32 (over z_hi, y, x).
Axes of the slice: x: 4, y: 4, z: 4 (z_hi: 2, z_lo: 2; z = z_hi * 2 + z_lo), core: 2. Of those that a mesh axis runs over, the one named last changes fastest.
Arguments:
- codes: bfloat16 [4, 32, 8192, 1024], P('ckpt', 'wide'), may hold values from -4 to 4
- scales: float32 [4, 32, 8192, 8], P('ckpt', 'wide'), may hold values from 0.5 to 5
- example_ids: int32 [32, 8192], P('wide'), may hold values from 0 to 8191, each once within a row
- targets: bfloat16 [4096, 4096], P('wide'), may hold values from -0.09375 to 0.09375
- owners: int32 [6], replicated, may hold values from 0 to 31, as said below
Outputs:
- scores: float32 [32, 8192, 768], P('wide', 'ckpt')
Inputs may be any that keep to these rules, and one draw needn't show every extreme that they name: `example_ids`: each row is a permutation of the 8192 examples of its group. Distinct owners; owner 0 and owner 32 - 1 are always among them.
All inputs are finite; a program needn't handle non-finite values.
Results may differ from a plain program's by a relative error of at most 0.0029.
Values may be sent and summed in bfloat16 or wider, within the bound.
No kernel may reach another device: no remote copies, remote signals or barrier semaphores. Data moves between devices by JAX's collectives and lax.ppermute only.
A program may use at most 192 MiB of HBM per device.

v0:
```python
import jax
import jax.numpy as jnp
from jax import lax
from jax.sharding import PartitionSpec as P


def from_root(shard, axis, root):
    mine = lax.axis_index(axis) == root
    return lax.psum(jnp.where(mine, shard, jnp.zeros_like(shard)), axis)


def fetch(targets, owner):
    whole = from_root(targets, "wide", owner)
    return whole


def per_device(codes, scales, example_ids, targets, owners):
    width = codes.shape[-1]
    block = width // scales.shape[-1]
    feats = (codes[0, 0].astype(jnp.float32) * jnp.repeat(scales[0, 0], block, axis=-1)).astype(
        jnp.bfloat16
    )
    ordered = jnp.take(feats, example_ids[0], axis=0)
    rounds = owners.shape[0]
    contract = (((1,), (1,)), ((), ()))
    resident = lax.all_to_all(ordered, "ckpt", split_axis=0, concat_axis=1, tiled=True)
    columns = []
    for step in range(rounds):
        chosen = fetch(targets, owners[step])
        columns.append(
            lax.dot_general(resident, chosen, contract, preferred_element_type=jnp.float32)
        )
    result = jnp.concatenate(columns, axis=1)
    scale_factor = 1.0 / lax.axis_size("ckpt")
    return (result * scale_factor)[None]


def solution(mesh):
    return jax.shard_map(
        per_device,
        mesh=mesh,
        in_specs=(
            P("ckpt", "wide", None, None),
            P("ckpt", "wide", None, None),
            P("wide", None),
            P("wide", None),
            P(),
        ),
        out_specs=P("wide", "ckpt", None),
        check_vma=False,
    )
```

profile of v0, /device:TPU:0, one launch (start us, length us, event | category | flops | bytes accessed | tf_op | source)
XLA Modules:
  0.0 588.3 jit_solution(14015166979742587643)
XLA Ops:
  6.5 3.5 copy.8
  10.1 0.8 compare_select_fusion
  10.9 10.3 %broadcast_in_dim.15 = f32[8192,8,128]{2,1,0:T(8,128)S(1)} broadcast(f32[8192,8]{1,0:T(8,128)} %copy.8), dimensions={0,1} | broadcast | bytes 33816576 | tf_op jit(solution)/shard_map/broadcast_in_dim | solution.py:20
  21.2 18.0 %fusion = bf16[8192,1024]{1,0:T(8,128)(2,1)} fusion(f32[1024,8,8,128]{3,2,1,0:T(8,128)S(1)} %bitcast.58, bf16[1,1,8192,1024]{3,2,1,0:T(8,128)(2,1)} %param.5), kind=kLoop, calls=%fused_computation.2 | loop fusion | flops 25165824 | bytes 67108864 | tf_op jit(solution)/shard_map/convert_element_type | solution.py:20
  39.1 48.6 %gather_fusion = bf16[8192,1024]{1,0:T(8,128)(2,1)} fusion(bf16[8192,1024]{1,0:T(8,128)(2,1)} %fusion, s32[8192]{0:T(1024)S(1)} %broadcast_clamp_fusion), kind=kCustom, calls=%fused_computation | custom fusion | bytes 33587200 | tf_op jit(solution)/shard_map/jit(_take)/gather | solution.py:23
  87.7 21.9 %copy.9 = bf16[4,2048,1024]{1,2,0:T(8,128)(2,1)} copy(bf16[4,2048,1024]{2,1,0:T(8,128)(2,1)} %bitcast.59) | data formatting | bytes 33554432 | tf_op jit(solution)/shard_map/jit(_take)/gather | solution.py:23
  109.5 0.5 broadcast.55
  110.1 0.7 reduce.3
  110.8 14.2 %broadcast_select_fusion = bf16[4,2048,1024]{1,2,0:T(8,128)(2,1)} fusion(bf16[4,2048,1024]{1,2,0:T(8,128)(2,1)} %copy.9, pred[4,2048]{1,0:T(4,128)(4,1)S(1)} %compare_and_fusion), kind=kLoop, calls=%fused_computation.3 | loop fusion | flops 8388608 | bytes 33562624 | tf_op jit(solution)/shard_map/jit(_take)/select_n | solution.py:23
  125.0 7.1 %all-to-all-start = ((bf16[4,2048,1024]{1,2,0:T(8,128)(2,1)}), bf16[4,2048,1024]{1,2,0:T(8,128)(2,1)}, u32[]{:S(2)}, u32[]{:S(2)}) async-start(bf16[4,2048,1024]{1,2,0:T(8,128)(2,1)} %broadcast_select_fusion), calls=%async_computation | async-start | bytes 33554432 | tf_op jit(solution)/shard_map/all_to_all | solution.py:26
  132.1 0.2 all-reduce.3.cloned.1.call-start
  132.4 0.7 fusion.7
  136.7 2.7 broadcast_select_fusion.1
  139.5 0.0 all-reduce.3.cloned.1.call-update
  139.5 382.1 %all-reduce.3.cloned.1.call-done = (bf16[128,4096]{1,0:T(8,128)(2,1)}, bf16[128,4096]{1,0:T(8,128)(2,1)}, bf16[128,4096]{1,0:T(8,128)(2,1)}, bf16[128,4096]{1,0:...) async-done(((bf16[128,4096]{1,0:T(8,128)(2,1)}, bf16[128,4096]{1,0:T(8,128)(2,1)}, bf16[128,4096]{1,0:T(8,128)(2,1)}, bf16[128,4096]{1,0:T(8,128)(2,1)}, ...) | async-done | bytes 6291472 | tf_op jit(solution)/shard_map/psum | solution.py:9
  521.6 0.0 all-to-all-done
  521.6 8.5 %fusion.6 = f32[1,2048,768]{1,2,0:T(8,128)S(1)} fusion(bf16[128,4096]{1,0:T(8,128)(2,1)} %get-tuple-element.5, bf16[2048,4096]{0,1:T(8,128)(2,1)} %bitcast.6), kind=kOutput, calls=%fused_computation.16 | convolution fusion | flops 2147483648 | bytes 18874368 | tf_op jit(solution)/shard_map/dot_general | solution.py:31
  530.1 8.2 %fusion.5 = f32[1,2048,768]{1,2,0:T(8,128)S(1)} fusion(f32[1,2048,768]{1,2,0:T(8,128)S(1)} %fusion.6, bf16[128,4096]{1,0:T(8,128)(2,1)S(1)} %copy-done.4, bf16[2048,4096]{0,1:T(8,128)(2,1)} %bitcast.6), kind=kOutput, calls=%fused_computation.14 | convolution fusion | flops 2147483648 | bytes 18874368 | tf_op jit(solution)/shard_map/dot_general | solution.py:31
  538.4 8.3 %fusion.4 = f32[1,2048,768]{1,2,0:T(8,128)S(1)} fusion(f32[1,2048,768]{1,2,0:T(8,128)S(1)} %fusion.5, bf16[128,4096]{1,0:T(8,128)(2,1)S(1)} %copy-done.3, bf16[2048,4096]{0,1:T(8,128)(2,1)} %bitcast.6), kind=kOutput, calls=%fused_computation.12 | convolution fusion | flops 2147483648 | bytes 18874368 | tf_op jit(solution)/shard_map/dot_general | solution.py:31
  546.6 8.3 %fusion.3 = f32[1,2048,768]{1,2,0:T(8,128)S(1)} fusion(f32[1,2048,768]{1,2,0:T(8,128)S(1)} %fusion.4, bf16[128,4096]{1,0:T(8,128)(2,1)S(1)} %copy-done.2, bf16[2048,4096]{0,1:T(8,128)(2,1)} %bitcast.6), kind=kOutput, calls=%fused_computation.10 | convolution fusion | flops 2147483648 | bytes 18874368 | tf_op jit(solution)/shard_map/dot_general | solution.py:31
  554.9 8.5 %fusion.2 = f32[1,2048,768]{1,2,0:T(8,128)S(1)} fusion(f32[1,2048,768]{1,2,0:T(8,128)S(1)} %fusion.3, bf16[128,4096]{1,0:T(8,128)(2,1)S(1)} %copy-done.1, bf16[2048,4096]{0,1:T(8,128)(2,1)} %bitcast.6), kind=kOutput, calls=%fused_computation.8 | convolution fusion | flops 2147483648 | bytes 18874368 | tf_op jit(solution)/shard_map/dot_general | solution.py:31
  563.5 8.2 %fusion.1 = f32[1,2048,768]{1,2,0:T(8,128)S(1)} fusion(f32[1,2048,768]{1,2,0:T(8,128)S(1)} %fusion.2, bf16[128,4096]{1,0:T(8,128)(2,1)S(1)} %copy-done, bf16[2048,4096]{0,1:T(8,128)(2,1)} %bitcast.6), kind=kOutput, calls=%fused_computation.6 | convolution fusion | flops 2147483648 | bytes 18874368 | tf_op jit(solution)/shard_map/dot_general | solution.py:31
  571.6 3.3 broadcast_multiply_fusion
  574.9 6.6 %copy.10 = f32[1,2048,768]{2,1,0:T(8,128)} copy(f32[1,2048,768]{1,2,0:T(8,128)} %broadcast_multiply_fusion) | data formatting | bytes 12582912 | tf_op jit(solution)/shard_map/mul | solution.py:35
  (19 shorter events, 0.1 us)
Async XLA Ops:
  87.7 22.4 %copy-start.6 = (s32[1,8192]{1,0:T(1,128)S(1)}, s32[1,8192]{1,0:T(1,128)}, u32[]{:S(2)}) copy-start(s32[1,8192]{1,0:T(1,128)} %param.7) | copy-start | bytes 98308
  125.0 7.4 %copy-start.7 = (s32[6]{0:T(128)S(1)}, s32[6]{0:T(128)}, u32[]{:S(2)}) copy-start(s32[6]{0:T(128)} %param.9) | copy-start | bytes 76
  125.0 11.7 %copy-start.5 = (bf16[128,4096]{1,0:T(8,128)(2,1)S(1)}, bf16[128,4096]{1,0:T(8,128)(2,1)}, u32[]{:S(2)}) copy-start(bf16[128,4096]{1,0:T(8,128)(2,1)} %param.8) | copy-start | bytes 3145732
  125.0 396.6 %all-to-all-start = ((bf16[4,2048,1024]{1,2,0:T(8,128)(2,1)}), bf16[4,2048,1024]{1,2,0:T(8,128)(2,1)}, u32[]{:S(2)}, u32[]{:S(2)}) async-start(bf16[4,2048,1024]{1,2,0:T(8,128)(2,1)} %broadcast_select_fusion), calls=%async_computation | async-start | bytes 33554432 | tf_op jit(solution)/shard_map/all_to_all | solution.py:26
  132.1 389.5 %all-reduce.3.cloned.1.call-start = ((), (), s32[]{:S(2)}) async-start(), calls=%async_computation.1 | async-start | bytes 12582912 | tf_op jit(solution)/shard_map/psum | solution.py:9
  521.6 8.5 %copy-start.4 = (bf16[128,4096]{1,0:T(8,128)(2,1)S(1)}, bf16[128,4096]{1,0:T(8,128)(2,1)}, u32[]{:S(2)}) copy-start(bf16[128,4096]{1,0:T(8,128)(2,1)} %get-tuple-element.6) | copy-start | bytes 3145732
  530.1 8.2 %copy-start.3 = (bf16[128,4096]{1,0:T(8,128)(2,1)S(1)}, bf16[128,4096]{1,0:T(8,128)(2,1)}, u32[]{:S(2)}) copy-start(bf16[128,4096]{1,0:T(8,128)(2,1)} %get-tuple-element.7) | copy-start | bytes 3145732
  538.3 8.3 %copy-start.2 = (bf16[128,4096]{1,0:T(8,128)(2,1)S(1)}, bf16[128,4096]{1,0:T(8,128)(2,1)}, u32[]{:S(2)}) copy-start(bf16[128,4096]{1,0:T(8,128)(2,1)} %get-tuple-element.8) | copy-start | bytes 3145732
  546.6 8.3 %copy-start.1 = (bf16[128,4096]{1,0:T(8,128)(2,1)S(1)}, bf16[128,4096]{1,0:T(8,128)(2,1)}, u32[]{:S(2)}) copy-start(bf16[128,4096]{1,0:T(8,128)(2,1)} %get-tuple-element.9) | copy-start | bytes 3145732
  554.9 8.5 %copy-start = (bf16[128,4096]{1,0:T(8,128)(2,1)S(1)}, bf16[128,4096]{1,0:T(8,128)(2,1)}, u32[]{:S(2)}) copy-start(bf16[128,4096]{1,0:T(8,128)(2,1)} %get-tuple-element.10) | copy-start | bytes 3145732
Sparse Core Ops, SparseCore 0:
  139.6 381.9 all-reduce.2
where the time goes:
time: 590 us; the launch traced here: 588 us
  waiting for transfers between devices  382 us (65%)
  local copies, waits for them, and re-layouts  92 us (16%)
  matrix products  49.9 us (8%)
  other arithmetic  39.7 us (7%)
  between operations  17.3 us (3%)
  starting transfers between devices  7.34 us (1%)
    psum x1, waiting for transfers between devices, from_root(): return lax.psum(jnp.where(mine, shard, jnp.zeros_like(shard)), axis)  382 us
    gather x2, local copies, waits for them, and re-layouts, per_device(): ordered = jnp.take(feats, example_ids[0], axis=0)  70.4 us
    dot_general x6, matrix products, per_device(): lax.dot_general(resident, chosen, contract, preferred_element_type=jnp.fl...  49.9 us
    convert_element_type x1, other arithmetic, per_device(): (codes[0, 0].astype(jnp.float32) * jnp.repeat(scales[0, 0], block, axis=-...  18 us
    select_n x2, other arithmetic, per_device(): ordered = jnp.take(feats, example_ids[0], axis=0)  14.9 us
  transfers between devices with their start and end apart: 2, of which 1 were waited for; matrix products, arithmetic and copies ran while one was open for 1% of the time, Pallas kernels for 0%

commit v1 on v0

v1 whole, which is shorter than its diff:
```python
import functools

import jax
import jax.numpy as jnp
from jax import lax
from jax.experimental import pallas as pl
from jax.experimental.pallas import tpu as pltpu
from jax.sharding import PartitionSpec as P

BF = jnp.bfloat16
F32 = jnp.float32
LANES = 128
PIECES = 8
TB = 128
RB = 512
VMEM = pl.BlockSpec(memory_space=pltpu.VMEM)
ANY = pl.BlockSpec(memory_space=pl.ANY)
NT = (((1,), (1,)), ((), ()))


def gather_body(parts, q_ref, ids_ref, codes_ref, sc_ref, *rest):
    outs = rest[: len(parts)]
    wide, held, stage, sem_in, sem_out = rest[len(parts) :]
    rows, width = held.shape
    nb = width // LANES
    piece = rows // PIECES
    quarter = rows // 4

    def load(i):
        at = pl.ds(i * piece, piece)
        return pltpu.make_async_copy(codes_ref.at[at], held.at[at], sem_in.at[i])

    for i in range(PIECES):
        load(i).start()
    spread = (
        lax.broadcasted_iota(jnp.int32, (3 * nb, width), 0) % nb
        == lax.broadcasted_iota(jnp.int32, (3 * nb, width), 1) // LANES
    ).astype(F32).astype(BF)
    for i in range(PIECES):
        load(i).wait()
        r0 = i * piece
        s = sc_ref[:, r0 : r0 + piece]
        hi = s.astype(BF)
        left = s - hi.astype(F32)
        mid = left.astype(BF)
        low = (left - mid.astype(F32)).astype(BF)
        three = jnp.concatenate([hi, mid, low], axis=0)
        scale = lax.dot_general(three, spread, (((0,), (0,)), ((), ())), preferred_element_type=F32)
        for b in range(nb):
            cols = slice(b * LANES, (b + 1) * LANES)
            wide[pl.ds(r0 * nb + b, piece, stride=nb), :] = (
                held[r0 : r0 + piece, cols].astype(F32) * scale[:, cols]
            )
    q = q_ref[0]
    for p, x in enumerate(parts):
        src = (q ^ x) * quarter

        def block(t, carry, p=p, src=src):
            o = pl.multiple_of(t * TB, TB)
            for r in range(TB):
                e = ids_ref[src + o + r]
                stage[r * nb : (r + 1) * nb, :] = wide[pl.ds(pl.multiple_of(e * nb, nb), nb), :]
            d = pl.multiple_of(p * quarter + o, TB)
            for b in range(nb):
                held[pl.ds(d, TB), b * LANES : (b + 1) * LANES] = stage[
                    pl.ds(b, TB, stride=nb), :
                ].astype(BF)
            pltpu.make_async_copy(
                held.at[pl.ds(d, TB)], outs[p].at[pl.ds(o, TB)], sem_out.at[p]
            ).start()
            return carry

        lax.fori_loop(0, quarter // TB, block, 0)
    for p in range(len(parts)):
        pltpu.make_async_copy(
            held.at[pl.ds(p * quarter, quarter)], outs[p], sem_out.at[p]
        ).wait()


def gather(parts, q, ids, codes, scales_t):
    rows, width = codes.shape
    nb = scales_t.shape[0]
    return pl.pallas_call(
        functools.partial(gather_body, parts),
        grid_spec=pltpu.PrefetchScalarGridSpec(
            num_scalar_prefetch=2,
            grid=(),
            in_specs=[ANY, VMEM],
            out_specs=[ANY] * len(parts),
            scratch_shapes=[
                pltpu.VMEM((rows * nb, LANES), F32),
                pltpu.VMEM((rows, width), BF),
                pltpu.VMEM((TB * nb, LANES), F32),
                pltpu.SemaphoreType.DMA((PIECES,)),
                pltpu.SemaphoreType.DMA((len(parts),)),
            ],
        ),
        out_shape=[jax.ShapeDtypeStruct((rows // 4, width), BF)] * len(parts),
        compiler_params=pltpu.CompilerParams(vmem_limit_bytes=58 * 1024 * 1024),
        cost_estimate=pl.CostEstimate(flops=40_000_000_000, bytes_accessed=50_000_000, transcendentals=0),
        name="gather_features",
    )(q, ids, codes, scales_t)


def pick_body(owners_ref, rec_ref, out_ref):
    n, rounds = out_ref.shape[:2]
    for r in range(rounds):
        piece = rec_ref[owners_ref[r]]
        for d in range(n):
            out_ref[d, r] = piece


def pick(owners, rec):
    n, h, w = rec.shape
    rounds = owners.shape[0]
    return pl.pallas_call(
        pick_body,
        grid_spec=pltpu.PrefetchScalarGridSpec(
            num_scalar_prefetch=1, grid=(), in_specs=[VMEM], out_specs=VMEM
        ),
        out_shape=jax.ShapeDtypeStruct((n, rounds, h, w), BF),
        name="pick_pieces",
    )(owners, rec)


def assemble(raw_ref, t_ref):
    n, rounds, h, w = raw_ref.shape
    cuts = t_ref.shape[1] // w
    for r in range(rounds):
        for g in range(n // cuts):
            for c in range(cuts):
                row = r * (n // cuts) * h + g * h
                t_ref[row : row + h, c * w : (c + 1) * w] = raw_ref[g * cuts + c, r]


def send_body(mine_ref, other_ref, tm_ref, to_ref, out_ref, tm, to):
    @pl.when(pl.program_id(0) == 0)
    def _():
        assemble(tm_ref, tm)
        assemble(to_ref, to)

    acc = lax.dot_general(mine_ref[...], tm[...], NT, preferred_element_type=F32)
    acc += lax.dot_general(other_ref[...], to[...], NT, preferred_element_type=F32)
    out_ref[...] = acc.astype(BF)


def final_body(scale, mine_ref, other_ref, tm_ref, to_ref, got_ref, prev_ref, out_ref, tm, to):
    @pl.when(pl.program_id(0) == 0)
    def _():
        assemble(tm_ref, tm)
        assemble(to_ref, to)

    acc = lax.dot_general(mine_ref[...], tm[...], NT, preferred_element_type=F32)
    acc += lax.dot_general(other_ref[...], to[...], NT, preferred_element_type=F32)
    out_ref[...] = (acc + got_ref[...].astype(F32)) * scale


def common_specs(mine, raw, first, count):
    rows, width = mine.shape
    n, _, h, w = raw.shape
    feats = pl.BlockSpec((RB, width), lambda i: (i, 0))
    targets = pl.BlockSpec((n, count, h, w), lambda i: (0, first // count, 0, 0))
    per_round = n * h * w // width
    scratch = [pltpu.VMEM((count * per_round, width), BF)] * 2
    return rows, count * per_round, [feats, feats, targets, targets], scratch


def send_scores(mine, other, raw_m, raw_o, first, count):
    rows, cols, specs, scratch = common_specs(mine, raw_m, first, count)
    return pl.pallas_call(
        send_body,
        grid=(rows // RB,),
        in_specs=specs,
        out_specs=pl.BlockSpec((RB, cols), lambda i: (i, 0)),
        scratch_shapes=scratch,
        out_shape=jax.ShapeDtypeStruct((rows, cols), BF),
        compiler_params=pltpu.CompilerParams(vmem_limit_bytes=32 * 1024 * 1024),
        name="send_scores",
    )(mine, other, raw_m, raw_o)


def final_scores(scale, mine, other, raw_m, raw_o, got, prev, first, count, total):
    rows, cols, specs, scratch = common_specs(mine, raw_m, first, count)
    if prev is None:
        prev, alias = jnp.zeros((8, LANES), F32), {}
    else:
        alias = {5: 0}
    return pl.pallas_call(
        functools.partial(final_body, scale),
        grid=(rows // RB,),
        in_specs=specs + [pl.BlockSpec((RB, cols), lambda i: (i, 0)), ANY],
        out_specs=pl.BlockSpec((RB, cols), lambda i: (i, first // count)),
        scratch_shapes=scratch,
        out_shape=jax.ShapeDtypeStruct((rows, total), F32),
        input_output_aliases=alias,
        compiler_params=pltpu.CompilerParams(vmem_limit_bytes=32 * 1024 * 1024),
        name="final_scores",
    )(mine, other, raw_m, raw_o, got, prev)


def per_device(codes, scales, example_ids, targets, owners):
    n_ckpt = lax.axis_size("ckpt")
    n_wide = lax.axis_size("wide")
    q = lax.axis_index("ckpt")
    width = codes.shape[-1]
    codes, scales_t, ids = codes[0, 0], scales[0, 0].T, example_ids[0]
    other_core = [(i, i ^ 1) for i in range(n_ckpt)]
    other_chip = [(i, i ^ 2) for i in range(n_ckpt)]

    cuts = 4
    rows = targets.shape[0]
    h, w = rows * cuts // n_wide, width // cuts
    own = lax.dynamic_slice_in_dim(targets, q * width, width, 1)
    pieces = own.reshape(n_wide // cuts, h, cuts, w).transpose(0, 2, 1, 3).reshape(n_wide, h, w)
    rec = lax.all_to_all(pieces, "wide", 0, 0, tiled=True)
    raw_m = lax.all_to_all(pick(owners, rec), "wide", 0, 0, tiled=True)
    raw_o = lax.ppermute(raw_m, "ckpt", other_core)

    q1 = q.reshape(1)
    to_partner_far, mine_far = gather((3, 2), q1, ids, codes, scales_t)
    other_far = lax.ppermute(to_partner_far, "ckpt", other_core)
    to_partner_near, mine_near = gather((1, 0), q1, ids, codes, scales_t)
    other_near = lax.ppermute(to_partner_near, "ckpt", other_core)

    rounds = owners.shape[0]
    count = 2
    got = []
    for first in range(0, rounds, count):
        part = send_scores(mine_far, other_far, raw_m, raw_o, first, count)
        got.append(lax.ppermute(part, "ckpt", other_chip))
    out = None
    for k, first in enumerate(range(0, rounds, count)):
        out = final_scores(
            1.0 / n_ckpt, mine_near, other_near, raw_m, raw_o, got[k], out, first, count, rounds * rows
        )
    return out[None]


def solution(mesh):
    return jax.shard_map(
        per_device,
        mesh=mesh,
        in_specs=(
            P("ckpt", "wide", None, None),
            P("ckpt", "wide", None, None),
            P("wide", None),
            P("wide", None),
            P(),
        ),
        out_specs=P("wide", "ckpt", None),
        check_vma=False,
    )
```

time: 590 us -> 178 us (0.30)
  waiting for transfers between devices: 382 us -> 48.7 us
  local copies, waits for them, and re-layouts: 92 us -> 5.05 us
  Pallas kernels: 0 us -> 74.5 us
  matrix products: 49.9 us -> 0 us
  other arithmetic: 39.7 us -> 0 us
  blocking collectives: 0 us -> 34 us
  between operations: 17.3 us -> 0.09 us
  starting transfers between devices: 7.34 us -> 14.8 us
    psum x1 -> x0, waiting for transfers between devices: 382 us -> none  [from_root(): return lax.psum(jnp.where(mine, shard, jnp.zeros_like(shard)), axis)]
    pallas_call x0 -> x9, Pallas kernels: none -> 74.5 us  [the longest x2 39.1 us: gather(): pl.pallas_call(functools.partial(gather_body, parts), grid_spec=pltpu.Pre...]
    gather x2 -> x0, local copies, waits for them, and re-layouts: 70.4 us -> none  [per_device(): ordered = jnp.take(feats, example_ids[0], axis=0)]
    dot_general x6 -> x0, matrix products: 49.9 us -> none  [per_device(): lax.dot_general(resident, chosen, contract, preferred_element_type=jnp.fl...]
    ppermute x0 -> x6, waiting for transfers between devices: none -> 48.7 us  [the longest x3 45.2 us: per_device(): got.append(lax.ppermute(part, 'ckpt', other_chip))]
    all_to_all x0 -> x1, blocking collectives: none -> 34 us  [per_device(): raw_m = lax.all_to_all(pick(owners, rec), 'wide', 0, 0, tiled=True)]
    convert_element_type x1 -> x0, other arithmetic: 18 us -> none  [per_device(): (codes[0, 0].astype(jnp.float32) * jnp.repeat(scales[0, 0], block, axis=-...]
    select_n x3 -> x0, other arithmetic: 17.7 us -> none  [the longest x2 14.9 us: per_device(): ordered = jnp.take(feats, example_ids[0], axis=0)]
  transfers between devices with their start and end apart: 2 -> 7, of which waited for: 1 -> 4; matrix products, arithmetic and copies ran while one was open for 1% -> 0% of each run, Pallas kernels for 0% -> 39%
where the time goes in v1:
time: 178 us; the launch traced here: 177 us
  Pallas kernels  74.5 us (42%)
  waiting for transfers between devices  48.7 us (27%)
  blocking collectives  34 us (19%)
  starting transfers between devices  14.8 us (8%)
  local copies, waits for them, and re-layouts  5.05 us (3%)
    ppermute x3, waiting for transfers between devices, per_device(): got.append(lax.ppermute(part, 'ckpt', other_chip))  45.2 us
    pallas_call x2, Pallas kernels, gather(): pl.pallas_call(functools.partial(gather_body, parts), grid_spec=pltpu.Pre...  39.1 us
    all_to_all x1, blocking collectives, per_device(): raw_m = lax.all_to_all(pick(owners, rec), 'wide', 0, 0, tiled=True)  34 us
    pallas_call x3, Pallas kernels, final_scores(): pl.pallas_call(functools.partial(final_body, scale), grid=(rows // RB,),...  17.6 us
    pallas_call x3, Pallas kernels, send_scores(): pl.pallas_call(send_body, grid=(rows // RB,), in_specs=specs, out_specs=p...  14.9 us
    all_to_all x1, starting transfers between devices, per_device(): rec = lax.all_to_all(pieces, 'wide', 0, 0, tiled=True)  10.7 us
    unnamed x8, local copies, waits for them, and re-layouts  4.12 us
  transfers between devices with their start and end apart: 7, of which 4 were waited for; matrix products, arithmetic and copies ran while one was open for 0% of the time, Pallas kernels for 39%

profile of v1, /device:TPU:0, one launch (start us, length us, event | category | flops | bytes accessed | tf_op | source)
XLA Modules:
  0.0 177.2 jit_solution(9335879010064878572)
XLA Ops:
  0.0 1.2 copy-done
  1.4 0.7 copy.8
  2.2 10.7 %all-to-all-start = ((bf16[32,16,256]{2,1,0:T(8,128)(2,1)}), bf16[32,16,256]{2,1,0:T(8,128)(2,1)S(1)}, u32[]{:S(2)}, u32[]{:S(2)}) async-start(bf16[32,16,256]{2,1,0:T(8,128)(2,1)} %bitcast.6), calls=%async_computation | async-start | bytes 524288 | tf_op jit(solution)/shard_map/all_to_all | solution.py:215
  12.9 19.6 %gather_features.3 = (bf16[2048,1024]{1,0:T(8,128)(2,1)}, bf16[2048,1024]{1,0:T(8,128)(2,1)}) custom-call(s32[1]{0:T(128)} %bitcast.q_ref, s32[8192]{0:T(1024)} %bitcast.14, bf16[8192,1024]{1,0:T(8,128)(2,1)} %bitcast.10, f32[8,8192]{1,0:T(8,128)} %bitcast.12), custom_call_target="tpu_custom_call" | custom-call | flops 40000000000 | bytes 50000000 | tf_op jit(solution)/shard_map/gather_features/pallas_call | solution.py:83
  32.5 0.3 collective-permute-start.2
  32.8 19.5 %gather_features.2 = (bf16[2048,1024]{1,0:T(8,128)(2,1)}, bf16[2048,1024]{1,0:T(8,128)(2,1)}) custom-call(s32[1]{0:T(128)} %bitcast.q_ref, s32[8192]{0:T(1024)} %bitcast.15, bf16[8192,1024]{1,0:T(8,128)(2,1)} %bitcast.11, f32[8,8192]{1,0:T(8,128)} %bitcast.13), custom_call_target="tpu_custom_call" | custom-call | flops 40000000000 | bytes 50000000 | tf_op jit(solution)/shard_map/gather_features/pallas_call | solution.py:83
  52.3 0.6 collective-permute-start
  52.9 0.7 copy-done.3
  53.6 3.0 %pick_pieces.1 = bf16[32,6,16,256]{3,2,1,0:T(8,128)(2,1)} custom-call(s32[6]{0:T(128)} %owners_ref.1, bf16[32,16,256]{2,1,0:T(8,128)(2,1)} %copy-done.3), custom_call_target="tpu_custom_call" | custom-call | tf_op jit(solution)/shard_map/pick_pieces/pallas_call | solution.py:116
  56.5 34.0 %all_to_all.10.tm_ref = bf16[32,6,16,256]{3,2,1,0:T(8,128)(2,1)S(1)} all-to-all(bf16[32,6,16,256]{3,2,1,0:T(8,128)(2,1)} %pick_pieces.1), channel_id=1, replica_groups=mesh['ckpt'=4,'wide'=32] {'wide'}, dimensions={0} | all-to-all | bytes 3145728 | tf_op jit(solution)/shard_map/all_to_all | solution.py:216
  90.6 3.4 %collective-permute-done.1.to_ref = bf16[32,6,16,256]{3,2,1,0:T(8,128)(2,1)S(1)} collective-permute-done((bf16[32,6,16,256]{3,2,1,0:T(8,128)(2,1)S(1)}, bf16[32,6,16,256]{3,2,1,0:T(8,128)(2,1)S(1)}, u32[]{:S(2)}, u32[]{:S(2)}) %collective-permute-start.1) | collective-permute-done | bytes 1572896 | tf_op jit(solution)/shard_map/ppermute | solution.py:217
  94.0 2.2 %copy-done.1 = bf16[2048,1024]{1,0:T(8,128)(2,1)S(1)} copy-done((bf16[2048,1024]{1,0:T(8,128)(2,1)S(1)}, bf16[2048,1024]{1,0:T(8,128)(2,1)}, u32[]{:S(2)}) %copy-start.1) | copy-done | bytes 4194328
  96.2 4.9 %send_scores.5 = bf16[2048,256]{1,0:T(8,128)(2,1)S(1)} custom-call(bf16[2048,1024]{1,0:T(8,128)(2,1)S(1)} %copy-done.1, bf16[2048,1024]{1,0:T(8,128)(2,1)} %collective-permute-done.2.other_ref, bf16[32,6,16,256]{3,2,1,0:T(8,128)(2,1)S(1)} %all_to_all.10.tm_ref, bf16[32,6,16,256]{3,2,1,0:T(8,128)(2,1)S(1)} %collective-permute-done.1.to_ref), custom_call_target="tpu_custom_call" | custom-call | tf_op jit(solution)/shard_map/send_scores/pallas_call | solution.py:170
  101.1 1.2 collective-permute-start.5
  102.2 4.9 %send_scores.4 = bf16[2048,256]{1,0:T(8,128)(2,1)S(1)} custom-call(bf16[2048,1024]{1,0:T(8,128)(2,1)S(1)} %copy-done.1, bf16[2048,1024]{1,0:T(8,128)(2,1)} %collective-permute-done.2.other_ref, bf16[32,6,16,256]{3,2,1,0:T(8,128)(2,1)S(1)} %all_to_all.10.tm_ref, bf16[32,6,16,256]{3,2,1,0:T(8,128)(2,1)S(1)} %collective-permute-done.1.to_ref), custom_call_target="tpu_custom_call" | custom-call | tf_op jit(solution)/shard_map/send_scores/pallas_call | solution.py:170
  107.1 1.0 collective-permute-start.4
  108.2 5.1 %send_scores.3 = bf16[2048,256]{1,0:T(8,128)(2,1)S(1)} custom-call(bf16[2048,1024]{1,0:T(8,128)(2,1)S(1)} %copy-done.1, bf16[2048,1024]{1,0:T(8,128)(2,1)} %collective-permute-done.2.other_ref, bf16[32,6,16,256]{3,2,1,0:T(8,128)(2,1)S(1)} %all_to_all.10.tm_ref, bf16[32,6,16,256]{3,2,1,0:T(8,128)(2,1)S(1)} %collective-permute-done.1.to_ref), custom_call_target="tpu_custom_call" | custom-call | tf_op jit(solution)/shard_map/send_scores/pallas_call | solution.py:170
  113.3 1.0 collective-permute-start.3
  114.3 12.8 %collective-permute-done.5.got_ref = bf16[2048,256]{1,0:T(8,128)(2,1)S(1)} collective-permute-done((bf16[2048,256]{1,0:T(8,128)(2,1)S(1)}, bf16[2048,256]{1,0:T(8,128)(2,1)S(1)}, u32[]{:S(2)}, u32[]{:S(2)}) %collective-permute-start.5) | collective-permute-done | bytes 1048608 | tf_op jit(solution)/shard_map/ppermute | solution.py:230
  127.2 5.9 %final_scores.3.prev_ref = f32[2048,768]{1,0:T(8,128)} custom-call(bf16[2048,1024]{1,0:T(8,128)(2,1)S(1)} %copy-done.2, bf16[2048,1024]{1,0:T(8,128)(2,1)} %collective-permute-done.other_ref, bf16[32,6,16,256]{3,2,1,0:T(8,128)(2,1)S(1)} %all_to_all.10.tm_ref, bf16[32,6,16,256]{3,2,1,0:T(8,128)(2,1)S(1)} %collective-permute-done.1.to_ref, ...), custom_call_target="tpu_custom_call" | custom-call | tf_op jit(solution)/shard_map/final_scores/pallas_call | solution.py:188
  133.0 16.6 %collective-permute-done.4.got_ref = bf16[2048,256]{1,0:T(8,128)(2,1)S(1)} collective-permute-done((bf16[2048,256]{1,0:T(8,128)(2,1)S(1)}, bf16[2048,256]{1,0:T(8,128)(2,1)S(1)}, u32[]{:S(2)}, u32[]{:S(2)}) %collective-permute-start.4) | collective-permute-done | bytes 1048608 | tf_op jit(solution)/shard_map/ppermute | solution.py:230
  149.6 5.9 %final_scores.4.prev_ref = f32[2048,768]{1,0:T(8,128)} custom-call(bf16[2048,1024]{1,0:T(8,128)(2,1)S(1)} %copy-done.2, bf16[2048,1024]{1,0:T(8,128)(2,1)} %collective-permute-done.other_ref, bf16[32,6,16,256]{3,2,1,0:T(8,128)(2,1)S(1)} %all_to_all.10.tm_ref, ...), custom_call_target="tpu_custom_call", output_to_operand_aliasing={{}: (5, {})} | custom-call | tf_op jit(solution)/shard_map/final_scores/pallas_call | solution.py:188
  155.5 15.8 %collective-permute-done.3.got_ref = bf16[2048,256]{1,0:T(8,128)(2,1)S(1)} collective-permute-done((bf16[2048,256]{1,0:T(8,128)(2,1)S(1)}, bf16[2048,256]{1,0:T(8,128)(2,1)S(1)}, u32[]{:S(2)}, u32[]{:S(2)}) %collective-permute-start.3) | collective-permute-done | bytes 1048608 | tf_op jit(solution)/shard_map/ppermute | solution.py:230
  171.3 5.9 %final_scores.5 = f32[2048,768]{1,0:T(8,128)} custom-call(bf16[2048,1024]{1,0:T(8,128)(2,1)S(1)} %copy-done.2, bf16[2048,1024]{1,0:T(8,128)(2,1)} %collective-permute-done.other_ref, bf16[32,6,16,256]{3,2,1,0:T(8,128)(2,1)S(1)} %all_to_all.10.tm_ref, bf16[32,6,16,256]{3,2,1,0:T(8,128)(2,1)S(1)} %collective-permute-done.1.to_ref, ...), custom_call_target="tpu_custom_call", output_to_operand_aliasing={{}: (5, {})} | custom-call | tf_op jit(solution)/shard_map/final_scores/pallas_call | solution.py:188
  (12 shorter events, 0.2 us)
Async XLA Ops:
  0.0 1.2 copy-start
  2.2 50.7 %all-to-all-start = ((bf16[32,16,256]{2,1,0:T(8,128)(2,1)}), bf16[32,16,256]{2,1,0:T(8,128)(2,1)S(1)}, u32[]{:S(2)}, u32[]{:S(2)}) async-start(bf16[32,16,256]{2,1,0:T(8,128)(2,1)} %bitcast.6), calls=%async_computation | async-start | bytes 524288 | tf_op jit(solution)/shard_map/all_to_all | solution.py:215
  32.5 61.5 %collective-permute-start.2 = (bf16[2048,1024]{1,0:T(8,128)(2,1)}, bf16[2048,1024]{1,0:T(8,128)(2,1)}, u32[]{:S(2)}, u32[]{:S(2)}) collective-permute-start(bf16[2048,1024]{1,0:T(8,128)(2,1)} %get-tuple-element.12), channel_id=1, source_target_pairs={{0,32},{32,0},{64,96},{96,64},{1,33},{33,1},{65,97},{97,65},{2,34}... | collective-permute-start | bytes 12582920 | tf_op jit(solution)/shard_map/ppermute | solution.py:221
  52.3 62.0 %collective-permute-start = (bf16[2048,1024]{1,0:T(8,128)(2,1)}, bf16[2048,1024]{1,0:T(8,128)(2,1)}, u32[]{:S(2)}, u32[]{:S(2)}) collective-permute-start(bf16[2048,1024]{1,0:T(8,128)(2,1)} %get-tuple-element.10), channel_id=1, source_target_pairs={{0,32},{32,0},{64,96},{96,64},{1,33},{33,1},{65,97},{97,65},{2,34}... | collective-permute-start | bytes 12582920 | tf_op jit(solution)/shard_map/ppermute | solution.py:223
  52.9 0.7 copy-start.3
  90.6 3.4 %collective-permute-start.1 = (bf16[32,6,16,256]{3,2,1,0:T(8,128)(2,1)S(1)}, bf16[32,6,16,256]{3,2,1,0:T(8,128)(2,1)S(1)}, u32[]{:S(2)}, u32[]{:S(2)}) collective-permute-start(bf16[32,6,16,256]{3,2,1,0:T(8,128)(2,1)S(1)} %all_to_all.10.tm_ref), channel_id=1, source_target_pairs={{0,32},{32,0},{64,96},{96,64},{1,33},{33,1},{65,97},{97,65},{2,34}... | collective-permute-start | bytes 4718600 | tf_op jit(solution)/shard_map/ppermute | solution.py:217
  94.0 2.2 %copy-start.1 = (bf16[2048,1024]{1,0:T(8,128)(2,1)S(1)}, bf16[2048,1024]{1,0:T(8,128)(2,1)}, u32[]{:S(2)}) copy-start(bf16[2048,1024]{1,0:T(8,128)(2,1)} %get-tuple-element.11.mine_ref) | copy-start | bytes 12582916
  101.1 26.1 %collective-permute-start.5 = (bf16[2048,256]{1,0:T(8,128)(2,1)S(1)}, bf16[2048,256]{1,0:T(8,128)(2,1)S(1)}, u32[]{:S(2)}, u32[]{:S(2)}) collective-permute-start(bf16[2048,256]{1,0:T(8,128)(2,1)S(1)} %send_scores.5), channel_id=1, source_target_pairs={{0,64},{32,96},{64,0},{96,32},{1,65},{33,97},{65,1},{97,33},{2,66}... | collective-permute-start | bytes 3145736 | tf_op jit(solution)/shard_map/ppermute | solution.py:230
  107.1 20.0 %copy-start.2 = (bf16[2048,1024]{1,0:T(8,128)(2,1)S(1)}, bf16[2048,1024]{1,0:T(8,128)(2,1)}, u32[]{:S(2)}) copy-start(bf16[2048,1024]{1,0:T(8,128)(2,1)} %get-tuple-element.9.mine_ref) | copy-start | bytes 12582916
  107.1 42.5 %collective-permute-start.4 = (bf16[2048,256]{1,0:T(8,128)(2,1)S(1)}, bf16[2048,256]{1,0:T(8,128)(2,1)S(1)}, u32[]{:S(2)}, u32[]{:S(2)}) collective-permute-start(bf16[2048,256]{1,0:T(8,128)(2,1)S(1)} %send_scores.4), channel_id=1, source_target_pairs={{0,64},{32,96},{64,0},{96,32},{1,65},{33,97},{65,1},{97,33},{2,66}... | collective-permute-start | bytes 3145736 | tf_op jit(solution)/shard_map/ppermute | solution.py:230
  113.3 58.0 %collective-permute-start.3 = (bf16[2048,256]{1,0:T(8,128)(2,1)S(1)}, bf16[2048,256]{1,0:T(8,128)(2,1)S(1)}, u32[]{:S(2)}, u32[]{:S(2)}) collective-permute-start(bf16[2048,256]{1,0:T(8,128)(2,1)S(1)} %send_scores.3), channel_id=1, source_target_pairs={{0,64},{32,96},{64,0},{96,32},{1,65},{33,97},{65,1},{97,33},{2,66}... | collective-permute-start | bytes 3145736 | tf_op jit(solution)/shard_map/ppermute | solution.py:230

commit v2 on v1

v2 whole, which is shorter than its diff:
```python
import functools

import jax
import jax.numpy as jnp
from jax import lax
from jax.experimental import pallas as pl
from jax.experimental.pallas import tpu as pltpu
from jax.sharding import PartitionSpec as P

BF = jnp.bfloat16
F32 = jnp.float32
I32 = jnp.int32
LANES = 128
PIECES = 8
TB = 128
CUTS = 4
MIB = 1024 * 1024
VMEM = pl.BlockSpec(memory_space=pltpu.VMEM)
SMEM = pl.BlockSpec(memory_space=pltpu.SMEM)
ANY = pl.BlockSpec(memory_space=pl.ANY)
NT = (((1,), (1,)), ((), ()))
TOKEN = jax.ShapeDtypeStruct((1,), I32)


def params(mib):
    return pltpu.CompilerParams(vmem_limit_bytes=mib * MIB)


def grid_of(scalars, grid, ins, outs, scratch=()):
    return pltpu.PrefetchScalarGridSpec(
        num_scalar_prefetch=scalars, grid=grid, in_specs=ins, out_specs=outs, scratch_shapes=scratch
    )


def gather_body(parts, q_ref, ids_ref, codes_ref, sc_ref, *rest):
    n = len(parts)
    outs, token = rest[:n], rest[n]
    wide, held, stage, sem_in, sem_out = rest[n + 1 :]
    rows, width = held.shape
    nb = width // LANES
    piece = rows // PIECES
    quarter = rows // 4

    def load(i):
        at = pl.ds(i * piece, piece)
        return pltpu.make_async_copy(codes_ref.at[at], held.at[at], sem_in.at[i])

    for i in range(PIECES):
        load(i).start()
    spread = (
        lax.broadcasted_iota(I32, (3 * nb, width), 0) % nb
        == lax.broadcasted_iota(I32, (3 * nb, width), 1) // LANES
    ).astype(F32).astype(BF)
    for i in range(PIECES):
        load(i).wait()
        r0 = i * piece
        s = sc_ref[:, r0 : r0 + piece]
        hi = s.astype(BF)
        left = s - hi.astype(F32)
        mid = left.astype(BF)
        low = (left - mid.astype(F32)).astype(BF)
        three = jnp.concatenate([hi, mid, low], axis=0)
        scale = lax.dot_general(three, spread, (((0,), (0,)), ((), ())), preferred_element_type=F32)
        for b in range(nb):
            cols = slice(b * LANES, (b + 1) * LANES)
            wide[pl.ds(r0 * nb + b, piece, stride=nb), :] = (
                held[r0 : r0 + piece, cols].astype(F32) * scale[:, cols]
            )
    q = q_ref[0]
    token[0] = q
    for p, x in enumerate(parts):
        src = (q ^ x) * quarter

        def block(t, carry, p=p, src=src):
            o = pl.multiple_of(t * TB, TB)
            for r in range(TB):
                e = ids_ref[src + o + r]
                stage[r * nb : (r + 1) * nb, :] = wide[pl.ds(pl.multiple_of(e * nb, nb), nb), :]
            d = pl.multiple_of(p * quarter + o, TB)
            for b in range(nb):
                held[pl.ds(d, TB), b * LANES : (b + 1) * LANES] = stage[
                    pl.ds(b, TB, stride=nb), :
                ].astype(BF)
            pltpu.make_async_copy(
                held.at[pl.ds(d, TB)], outs[p].at[pl.ds(o, TB)], sem_out.at[p]
            ).start()
            return carry

        lax.fori_loop(0, quarter // TB, block, 0)
    for p in range(n):
        pltpu.make_async_copy(
            held.at[pl.ds(p * quarter, quarter)], outs[p], sem_out.at[p]
        ).wait()


def gather(parts, q, ids, codes, scales_t):
    rows, width = codes.shape
    nb = scales_t.shape[0]
    n = len(parts)
    return pl.pallas_call(
        functools.partial(gather_body, parts),
        grid_spec=grid_of(
            2,
            (),
            [ANY, VMEM],
            [ANY] * n + [SMEM],
            [
                pltpu.VMEM((rows * nb, LANES), F32),
                pltpu.VMEM((rows, width), BF),
                pltpu.VMEM((TB * nb, LANES), F32),
                pltpu.SemaphoreType.DMA((PIECES,)),
                pltpu.SemaphoreType.DMA((n,)),
            ],
        ),
        out_shape=[jax.ShapeDtypeStruct((rows // 4, width), BF)] * n + [TOKEN],
        compiler_params=params(54),
        name="gather_features",
    )(q, ids, codes, scales_t)


def pick_body(owners_ref, q_ref, rec_ref, held_ref, out_ref, token, held_out):
    token[0] = q_ref[0]
    n, rounds = out_ref.shape[:2]
    for r in range(rounds):
        piece = rec_ref[owners_ref[r]]
        for d in range(n):
            out_ref[d, r] = piece


def pick(owners, q, rec, held):
    n, h, w = rec.shape
    return pl.pallas_call(
        pick_body,
        grid_spec=grid_of(2, (), [VMEM, ANY], [VMEM, SMEM, ANY]),
        out_shape=[
            jax.ShapeDtypeStruct((n, owners.shape[0], h, w), BF),
            TOKEN,
            jax.ShapeDtypeStruct(held.shape, held.dtype),
        ],
        input_output_aliases={3: 2},
        compiler_params=params(8),
        name="pick_pieces",
    )(owners, q, rec, held)


def tie_body(q_ref, x_ref, y_ref, x_out, y_out, token):
    token[0] = q_ref[0]


def tie(q, x, y):
    return pl.pallas_call(
        tie_body,
        grid_spec=grid_of(1, (), [ANY, ANY], [ANY, ANY, SMEM]),
        out_shape=[jax.ShapeDtypeStruct(a.shape, a.dtype) for a in (x, y)] + [TOKEN],
        input_output_aliases={1: 0, 2: 1},
        compiler_params=params(56),
        name="tie",
    )(q, x, y)


def lay(raw_ref, t_ref):
    n, rounds, h, w = raw_ref.shape
    per = t_ref.shape[0] // rounds
    for r in range(rounds):
        for d in range(n):
            row = r * per + d // CUTS * h
            t_ref[row : row + h, d % CUTS * w : (d % CUTS + 1) * w] = raw_ref[d, r]


def dots(mine_ref, other_ref, tm, to):
    acc = lax.dot_general(mine_ref[...], tm[...], NT, preferred_element_type=F32)
    return acc + lax.dot_general(other_ref[...], to[...], NT, preferred_element_type=F32)


def send_body(q_ref, mine_ref, other_ref, tm_ref, to_ref, *rest):
    out_ref, token, tm, to = rest[-4:]
    token[0] = q_ref[0]

    @pl.when(pl.program_id(0) == 0)
    def _():
        lay(tm_ref, tm)
        lay(to_ref, to)

    out_ref[...] = dots(mine_ref, other_ref, tm, to).astype(BF)


def send_scores(q, mine, other, raw_m, raw_o, pair, per, start, count, after=(), block=512):
    width = mine.shape[1]
    n, _, h, w = raw_m.shape
    feats = pl.BlockSpec((block, width), lambda i, *_: (i + start // block, 0))
    targets = pl.BlockSpec((n, 2, h, w), lambda i, *_: (0, pair, 0, 0))
    return pl.pallas_call(
        send_body,
        grid_spec=grid_of(
            1,
            (count // block,),
            [feats, feats, targets, targets] + [ANY] * len(after),
            [pl.BlockSpec((block, 2 * per), lambda i, *_: (i, 0)), SMEM],
            [pltpu.VMEM((2 * per, width), BF)] * 2,
        ),
        out_shape=[jax.ShapeDtypeStruct((count, 2 * per), BF), TOKEN],
        compiler_params=params(16),
        name="send_scores",
    )(q, mine, other, raw_m, raw_o, *after)


def near_body(scale, q_ref, mine_ref, other_ref, tm_ref, to_ref, out_ref, tm, to):
    @pl.when(pl.program_id(0) == 0)
    def _():
        lay(tm_ref, tm)
        lay(to_ref, to)

    out_ref[...] = dots(mine_ref, other_ref, tm, to) * scale


def near_scores(q, scale, mine, other, raw_m, raw_o, per, block=256):
    rows, width = mine.shape
    total = per * raw_m.shape[1]
    feats = pl.BlockSpec((block, width), lambda i, *_: (i, 0))
    raw = pl.BlockSpec(raw_m.shape, lambda i, *_: (0, 0, 0, 0))
    return pl.pallas_call(
        functools.partial(near_body, scale),
        grid_spec=grid_of(
            1,
            (rows // block,),
            [feats, feats, raw, raw],
            pl.BlockSpec((block, total), lambda i, *_: (i, 0)),
            [pltpu.VMEM((total, width), BF)] * 2,
        ),
        out_shape=jax.ShapeDtypeStruct((rows, total), F32),
        compiler_params=params(32),
        name="near_scores",
    )(q, mine, other, raw_m, raw_o)


def add_body(scale, got_ref, old_ref, out_ref):
    out_ref[...] = old_ref[...] + got_ref[...].astype(F32) * scale


def add_scores(scale, got, out, pair, start, block=512):
    count, cols = got.shape
    cell = pl.BlockSpec((block, cols), lambda i: (i + start // block, pair))
    return pl.pallas_call(
        functools.partial(add_body, scale),
        grid=(count // block,),
        in_specs=[pl.BlockSpec((block, cols), lambda i: (i, 0)), cell],
        out_specs=cell,
        out_shape=jax.ShapeDtypeStruct(out.shape, F32),
        input_output_aliases={1: 0},
        compiler_params=params(16),
        name="add_scores",
    )(got, out)


def per_device(codes, scales, example_ids, targets, owners):
    n_ckpt = lax.axis_size("ckpt")
    n_wide = lax.axis_size("wide")
    q = lax.axis_index("ckpt")
    width = codes.shape[-1]
    codes, scales_t, ids = codes[0, 0], scales[0, 0].T, example_ids[0]
    other_core = [(i, i ^ 1) for i in range(n_ckpt)]
    other_chip = [(i, i ^ 2) for i in range(n_ckpt)]
    per = targets.shape[0]
    quarter = ids.shape[0] // n_ckpt
    scale = 1.0 / n_ckpt
    q1 = q.reshape(1)

    h, w = per * CUTS // n_wide, width // CUTS
    own = lax.dynamic_slice_in_dim(targets, q * width, width, 1)
    pieces = own.reshape(n_wide // CUTS, h, CUTS, w).transpose(0, 2, 1, 3).reshape(n_wide, h, w)
    rec = lax.all_to_all(pieces, "wide", 0, 0, tiled=True)
    to_far, tok = gather((3,), q1, ids, codes, scales_t)

    picked, tok, to_far = pick(owners, tok, rec, to_far)
    other_far = lax.ppermute(to_far, "ckpt", other_core)
    raw_m = lax.all_to_all(picked, "wide", 0, 0, tiled=True)
    mine_far, to_near, mine_near, tok = gather((2, 1, 0), tok, ids, codes, scales_t)
    raw_m, to_near, tok = tie(tok, raw_m, to_near)
    raw_o = lax.ppermute(raw_m, "ckpt", other_core)

    other_near = lax.ppermute(to_near, "ckpt", other_core)

    sent = []
    for pair, start, count in plan(owners.shape[0] // 2, quarter):
        after = [sent[-3][0]] if len(sent) > 2 else []
        part, tok = send_scores(
            tok, mine_far, other_far, raw_m, raw_o, pair, per, start, count, after
        )
        sent.append((lax.ppermute(part, "ckpt", other_chip), pair, start))

    out = near_scores(tok, scale, mine_near, other_near, raw_m, raw_o, per)
    for got, pair, start in sent:
        out = add_scores(scale, got, out, pair, start)
    return out[None]


def plan(pairs, rows):
    for pair in range(pairs):
        cuts = 2 if pair in (0, pairs - 1) else 1
        for c in range(cuts):
            yield pair, c * (rows // cuts), rows // cuts


def solution(mesh):
    return jax.shard_map(
        per_device,
        mesh=mesh,
        in_specs=(
            P("ckpt", "wide", None, None),
            P("ckpt", "wide", None, None),
            P("wide", None),
            P("wide", None),
            P(),
        ),
        out_specs=P("wide", "ckpt", None),
        check_vma=False,
    )
```

time: 178 us -> 163 us (0.916)
  blocking collectives: 34 us -> 0 us
  starting transfers between devices: 14.8 us -> 27.2 us
  Pallas kernels: 74.5 us -> 86.3 us
  waiting for transfers between devices: 48.7 us -> 37.4 us
  local copies, waits for them, and re-layouts: 5.05 us -> 10.1 us
    all_to_all x1 -> x0, blocking collectives: 34 us -> none  [per_device(): raw_m = lax.all_to_all(pick(owners, rec), 'wide', 0, 0, tiled=True)]
    ppermute x5 -> x7, waiting for transfers between devices: 45.3 us -> 28.3 us  [the longest x5 28.3 us: per_device(): sent.append((lax.ppermute(part, 'ckpt', other_chip), pair, start))]
    pallas_call x9 -> x15, Pallas kernels: 74.5 us -> 86.3 us  [the longest x2 40.9 us: gather(): pl.pallas_call(functools.partial(gather_body, parts), grid_spec=grid_of(2...]
    all_to_all x0 -> x1, starting transfers between devices: none -> 9.83 us  [per_device(): raw_m = lax.all_to_all(picked, 'wide', 0, 0, tiled=True)]
    ppermute x1, waiting for transfers between devices: 3.41 us -> 9.15 us  [per_device(): raw_o = lax.ppermute(raw_m, 'ckpt', other_core)]
    unnamed x8 -> x20, local copies, waits for them, and re-layouts: 4.12 us -> 9.2 us
    ppermute x5 -> x7, starting transfers between devices: 4.07 us -> 6.55 us  [the longest x5 5.72 us: per_device(): sent.append((lax.ppermute(part, 'ckpt', other_chip), pair, start))]
  transfers between devices with their start and end apart: 7 -> 10, of which waited for: 4 -> 6; matrix products, arithmetic and copies ran while one was open for 0% -> 0% of each run, Pallas kernels for 39% -> 51%
where the time goes in v2:
time: 163 us; the launch traced here: 161 us
  Pallas kernels  86.3 us (53%)
  waiting for transfers between devices  37.4 us (23%)
  starting transfers between devices  27.2 us (17%)
  local copies, waits for them, and re-layouts  10.1 us (6%)
    pallas_call x2, Pallas kernels, gather(): pl.pallas_call(functools.partial(gather_body, parts), grid_spec=grid_of(2...  40.9 us
    ppermute x5, waiting for transfers between devices, per_device(): sent.append((lax.ppermute(part, 'ckpt', other_chip), pair, start))  28.3 us
    pallas_call x5, Pallas kernels, send_scores(): pl.pallas_call(send_body, grid_spec=grid_of(1, (count // block,), [feats,...  20 us
    pallas_call x5, Pallas kernels, add_scores(): pl.pallas_call(functools.partial(add_body, scale), grid=(count // block,)...  12.1 us
    all_to_all x1, starting transfers between devices, per_device(): rec = lax.all_to_all(pieces, 'wide', 0, 0, tiled=True)  10.7 us
    pallas_call x1, Pallas kernels, near_scores(): pl.pallas_call(functools.partial(near_body, scale), grid_spec=grid_of(1,...  9.86 us
    all_to_all x1, starting transfers between devices, per_device(): raw_m = lax.all_to_all(picked, 'wide', 0, 0, tiled=True)  9.83 us
    unnamed x20, local copies, waits for them, and re-layouts  9.2 us
  transfers between devices with their start and end apart: 10, of which 6 were waited for; matrix products, arithmetic and copies ran while one was open for 0% of the time, Pallas kernels for 51%

profile of v2, /device:TPU:0, one launch (start us, length us, event | category | flops | bytes accessed | tf_op | source)
XLA Modules:
  0.0 161.2 jit_solution(858290276995787275)
XLA Ops:
  2.2 10.7 %all-to-all-start = ((bf16[32,16,256]{2,1,0:T(8,128)(2,1)}), bf16[32,16,256]{2,1,0:T(8,128)(2,1)S(1)}, u32[]{:S(2)}, u32[]{:S(2)}) async-start(bf16[32,16,256]{2,1,0:T(8,128)(2,1)} %bitcast.6), calls=%async_computation | async-start | bytes 524288 | tf_op jit(solution)/shard_map/all_to_all | solution.py:271
  12.9 16.6 %gather_features.2 = (bf16[2048,1024]{1,0:T(8,128)(2,1)}, s32[1]{0:T(128)}) custom-call(s32[1]{0:T(128)} %bitcast.q_ref, s32[8192]{0:T(1024)} %bitcast.14, bf16[8192,1024]{1,0:T(8,128)(2,1)} %bitcast.9, f32[8,8192]{1,0:T(8,128)} %bitcast.11), custom_call_target="tpu_custom_call" | custom-call | tf_op jit(solution)/shard_map/gather_features/pallas_call | solution.py:100
  29.5 2.2 %copy-done.6 = bf16[2048,1024]{1,0:T(8,128)(2,1)S(1)} copy-done((bf16[2048,1024]{1,0:T(8,128)(2,1)S(1)}, bf16[2048,1024]{1,0:T(8,128)(2,1)}, u32[]{:S(2)}) %copy-start.6) | copy-done | bytes 4194328
  33.3 2.0 %copy-done.7 = bf16[2048,1024]{1,0:T(8,128)(2,1)} copy-done((bf16[2048,1024]{1,0:T(8,128)(2,1)}, bf16[2048,1024]{1,0:T(8,128)(2,1)S(1)}, u32[]{:S(2)}) %copy-start.7) | copy-done | bytes 4194328
  36.5 9.8 %all-to-all-start.1 = ((bf16[32,6,16,256]{3,2,1,0:T(8,128)(2,1)}), bf16[32,6,16,256]{3,2,1,0:T(8,128)(2,1)S(1)}, u32[]{:S(2)}, u32[]{:S(2)}) async-start(bf16[32,6,16,256]{3,2,1,0:T(8,128)(2,1)} %copy-done.8), calls=%async_computation.1 | async-start | bytes 3145728 | tf_op jit(solution)/shard_map/all_to_all | solution.py:276
  46.6 24.3 %gather_features.3 = (bf16[2048,1024]{1,0:T(8,128)(2,1)}, bf16[2048,1024]{1,0:T(8,128)(2,1)}, bf16[2048,1024]{1,0:T(8,128)(2,1)}, s32[1]{0:T(128)}) custom-call(s32[1]{0:T(128)} %get-tuple-element.29.q_ref, s32[8192]{0:T(1024)} %bitcast.15, bf16[8192,1024]{1,0:T(8,128)(2,1)} %bitcast.10, f32[8,8192]{1,0:T(8,128)} %bitcast.12), custom_call_target="tpu_custom_call" | custom-call | tf_op jit(solution)/shard_map/gather_features/pallas_call | solution.py:100
  72.1 1.8 %tie.1 = (bf16[32,6,16,256]{3,2,1,0:T(8,128)(2,1)}, bf16[2048,1024]{1,0:T(8,128)(2,1)}, s32[1]{0:T(128)}) custom-call(s32[1]{0:T(128)} %get-tuple-element.30.q_ref, bf16[32,6,16,256]{3,2,1,0:T(8,128)(2,1)} %copy-done.2, bf16[2048,1024]{1,0:T(8,128)(2,1)} %get-tuple-element.32.y_ref), custom_call_target="tpu_custom_call", output_to_operand_aliasing={{0}: (1, {}), {1}: (2, {})} | custom-call | tf_op jit(solution)/shard_map/tie/pallas_call | solution.py:151
  74.6 9.2 %collective-permute-done.1.to_ref = bf16[32,6,16,256]{3,2,1,0:T(8,128)(2,1)S(1)} collective-permute-done((bf16[32,6,16,256]{3,2,1,0:T(8,128)(2,1)}, bf16[32,6,16,256]{3,2,1,0:T(8,128)(2,1)S(1)}, u32[]{:S(2)}, u32[]{:S(2)}) %collective-permute-start.1) | collective-permute-done | bytes 1572896 | tf_op jit(solution)/shard_map/ppermute | solution.py:279
  85.2 3.5 %send_scores.5 = (bf16[1024,256]{1,0:T(8,128)(2,1)S(1)}, s32[1]{0:T(128)}) custom-call(s32[1]{0:T(128)} %get-tuple-element.33.q_ref, bf16[2048,1024]{1,0:T(8,128)(2,1)S(1)} %copy-done.1, bf16[2048,1024]{1,0:T(8,128)(2,1)} %collective-permute-done.other_ref, bf16[32,6,16,256]{3,2,1,0:T(8,128)(2,1)S(1)} %copy-done.3, ...), custom_call_target="tpu_custom_call" | custom-call | tf_op jit(solution)/shard_map/send_scores/pallas_call | solution.py:192
  89.8 3.5 %send_scores.6 = (bf16[1024,256]{1,0:T(8,128)(2,1)S(1)}, s32[1]{0:T(128)}) custom-call(s32[1]{0:T(128)} %get-tuple-element.37.q_ref, bf16[2048,1024]{1,0:T(8,128)(2,1)S(1)} %copy-done.1, bf16[2048,1024]{1,0:T(8,128)(2,1)} %collective-permute-done.other_ref, bf16[32,6,16,256]{3,2,1,0:T(8,128)(2,1)S(1)} %copy-done.3, ...), custom_call_target="tpu_custom_call" | custom-call | tf_op jit(solution)/shard_map/send_scores/pallas_call | solution.py:192
  94.4 5.5 %send_scores.7 = (bf16[2048,256]{1,0:T(8,128)(2,1)S(1)}, s32[1]{0:T(128)}) custom-call(s32[1]{0:T(128)} %get-tuple-element.38.q_ref, bf16[2048,1024]{1,0:T(8,128)(2,1)S(1)} %copy-done.1, bf16[2048,1024]{1,0:T(8,128)(2,1)} %collective-permute-done.other_ref, bf16[32,6,16,256]{3,2,1,0:T(8,128)(2,1)S(1)} %copy-done.3, ...), custom_call_target="tpu_custom_call" | custom-call | tf_op jit(solution)/shard_map/send_scores/pallas_call | solution.py:192
  101.0 2.5 %collective-permute-done.2.rest_0_.got_ref = bf16[1024,256]{1,0:T(8,128)(2,1)S(1)} collective-permute-done((bf16[1024,256]{1,0:T(8,128)(2,1)S(1)}, bf16[1024,256]{1,0:T(8,128)(2,1)S(1)}, u32[]{:S(2)}, u32[]{:S(2)}) %collective-permute-start.2) | collective-permute-done | bytes 524320 | tf_op jit(solution)/shard_map/ppermute | solution.py:289
  103.5 3.5 %send_scores.8 = (bf16[1024,256]{1,0:T(8,128)(2,1)S(1)}, s32[1]{0:T(128)}) custom-call(s32[1]{0:T(128)} %get-tuple-element.39.q_ref, bf16[2048,1024]{1,0:T(8,128)(2,1)S(1)} %copy-done.1, bf16[2048,1024]{1,0:T(8,128)(2,1)} %collective-permute-done.other_ref, bf16[32,6,16,256]{3,2,1,0:T(8,128)(2,1)S(1)} %copy-done.3, ...), custom_call_target="tpu_custom_call" | custom-call | tf_op jit(solution)/shard_map/send_scores/pallas_call | solution.py:192
  108.4 6.4 %collective-permute-done.3.rest_0_.got_ref = bf16[1024,256]{1,0:T(8,128)(2,1)S(1)} collective-permute-done((bf16[1024,256]{1,0:T(8,128)(2,1)S(1)}, bf16[1024,256]{1,0:T(8,128)(2,1)S(1)}, u32[]{:S(2)}, u32[]{:S(2)}) %collective-permute-start.3) | collective-permute-done | bytes 524320 | tf_op jit(solution)/shard_map/ppermute | solution.py:289
  114.8 4.0 %send_scores.9 = (bf16[1024,256]{1,0:T(8,128)(2,1)S(1)}, s32[1]{0:T(128)}) custom-call(s32[1]{0:T(128)} %get-tuple-element.41.q_ref, bf16[2048,1024]{1,0:T(8,128)(2,1)S(1)} %copy-done.1, bf16[2048,1024]{1,0:T(8,128)(2,1)} %collective-permute-done.other_ref, bf16[32,6,16,256]{3,2,1,0:T(8,128)(2,1)S(1)} %copy-done.3, ...), custom_call_target="tpu_custom_call" | custom-call | tf_op jit(solution)/shard_map/send_scores/pallas_call | solution.py:192
  119.9 9.9 %near_scores.1.old_ref = f32[2048,768]{1,0:T(8,128)} custom-call(s32[1]{0:T(128)} %get-tuple-element.46.q_ref, bf16[2048,1024]{1,0:T(8,128)(2,1)S(1)} %copy-done.5, bf16[2048,1024]{1,0:T(8,128)(2,1)S(1)} %collective-permute-done.7.other_ref, bf16[32,6,16,256]{3,2,1,0:T(8,128)(2,1)S(1)} %copy-done.4, bf16[32,6,16,256]{3,2,1,0:T(8,128)(2,1)S(1)} %collective-permute-done.1.to_ref), custom_call_target="tpu_custom_call" | custom-call | tf_op jit(solution)/shard_map/near_scores/pallas_call | solution.py:221
  129.8 2.1 %add_scores.5.old_ref = f32[2048,768]{1,0:T(8,128)} custom-call(bf16[1024,256]{1,0:T(8,128)(2,1)S(1)} %collective-permute-done.2.rest_0_.got_ref, f32[2048,768]{1,0:T(8,128)} %near_scores.1.old_ref), custom_call_target="tpu_custom_call", output_to_operand_aliasing={{}: (1, {})} | custom-call | tf_op jit(solution)/shard_map/add_scores/pallas_call | solution.py:243
  131.9 2.1 %add_scores.6.old_ref = f32[2048,768]{1,0:T(8,128)} custom-call(bf16[1024,256]{1,0:T(8,128)(2,1)S(1)} %collective-permute-done.3.rest_0_.got_ref, f32[2048,768]{1,0:T(8,128)} %add_scores.5.old_ref), custom_call_target="tpu_custom_call", output_to_operand_aliasing={{}: (1, {})} | custom-call | tf_op jit(solution)/shard_map/add_scores/pallas_call | solution.py:243
  133.9 3.3 %collective-permute-done.6.got_ref = bf16[2048,256]{1,0:T(8,128)(2,1)S(1)} collective-permute-done((bf16[2048,256]{1,0:T(8,128)(2,1)S(1)}, bf16[2048,256]{1,0:T(8,128)(2,1)S(1)}, u32[]{:S(2)}, u32[]{:S(2)}) %collective-permute-start.6) | collective-permute-done | bytes 1048608 | tf_op jit(solution)/shard_map/ppermute | solution.py:289
  137.2 3.8 %add_scores.7.old_ref = f32[2048,768]{1,0:T(8,128)} custom-call(bf16[2048,256]{1,0:T(8,128)(2,1)S(1)} %collective-permute-done.6.got_ref, f32[2048,768]{1,0:T(8,128)} %add_scores.6.old_ref), custom_call_target="tpu_custom_call", output_to_operand_aliasing={{}: (1, {})} | custom-call | tf_op jit(solution)/shard_map/add_scores/pallas_call | solution.py:243
  141.1 7.4 %collective-permute-done.5.got_ref = bf16[1024,256]{1,0:T(8,128)(2,1)S(1)} collective-permute-done((bf16[1024,256]{1,0:T(8,128)(2,1)S(1)}, bf16[1024,256]{1,0:T(8,128)(2,1)S(1)}, u32[]{:S(2)}, u32[]{:S(2)}) %collective-permute-start.5) | collective-permute-done | bytes 524320 | tf_op jit(solution)/shard_map/ppermute | solution.py:289
  148.5 2.1 %add_scores.8.old_ref = f32[2048,768]{1,0:T(8,128)} custom-call(bf16[1024,256]{1,0:T(8,128)(2,1)S(1)} %collective-permute-done.5.got_ref, f32[2048,768]{1,0:T(8,128)} %add_scores.7.old_ref), custom_call_target="tpu_custom_call", output_to_operand_aliasing={{}: (1, {})} | custom-call | tf_op jit(solution)/shard_map/add_scores/pallas_call | solution.py:243
  150.5 8.6 %collective-permute-done.4.got_ref = bf16[1024,256]{1,0:T(8,128)(2,1)S(1)} collective-permute-done((bf16[1024,256]{1,0:T(8,128)(2,1)S(1)}, bf16[1024,256]{1,0:T(8,128)(2,1)S(1)}, u32[]{:S(2)}, u32[]{:S(2)}) %collective-permute-start.4) | collective-permute-done | bytes 524320 | tf_op jit(solution)/shard_map/ppermute | solution.py:289
  159.2 2.1 %add_scores.9 = f32[2048,768]{1,0:T(8,128)} custom-call(bf16[1024,256]{1,0:T(8,128)(2,1)S(1)} %collective-permute-done.4.got_ref, f32[2048,768]{1,0:T(8,128)} %add_scores.8.old_ref), custom_call_target="tpu_custom_call", output_to_operand_aliasing={{}: (1, {})} | custom-call | tf_op jit(solution)/shard_map/add_scores/pallas_call | solution.py:243
  (34 shorter events, 14.2 us)
Async XLA Ops:
  0.0 1.2 copy-start
  2.2 27.3 %all-to-all-start = ((bf16[32,16,256]{2,1,0:T(8,128)(2,1)}), bf16[32,16,256]{2,1,0:T(8,128)(2,1)S(1)}, u32[]{:S(2)}, u32[]{:S(2)}) async-start(bf16[32,16,256]{2,1,0:T(8,128)(2,1)} %bitcast.6), calls=%async_computation | async-start | bytes 524288 | tf_op jit(solution)/shard_map/all_to_all | solution.py:271
  12.9 16.6 %copy-start.9 = (s32[6]{0:T(128)S(1)}, s32[6]{0:T(128)}, u32[]{:S(2)}) copy-start(s32[6]{0:T(128)} %owners_ref.1) | copy-start | bytes 76
  29.5 2.2 %copy-start.6 = (bf16[2048,1024]{1,0:T(8,128)(2,1)S(1)}, bf16[2048,1024]{1,0:T(8,128)(2,1)}, u32[]{:S(2)}) copy-start(bf16[2048,1024]{1,0:T(8,128)(2,1)} %get-tuple-element.28.held_ref) | copy-start | bytes 12582916
  33.3 2.0 %copy-start.7 = (bf16[2048,1024]{1,0:T(8,128)(2,1)}, bf16[2048,1024]{1,0:T(8,128)(2,1)S(1)}, u32[]{:S(2)}) copy-start(bf16[2048,1024]{1,0:T(8,128)(2,1)S(1)} %get-tuple-element.35) | copy-start | bytes 12582916
  35.3 1.2 copy-start.8
  36.5 34.4 %all-to-all-start.1 = ((bf16[32,6,16,256]{3,2,1,0:T(8,128)(2,1)}), bf16[32,6,16,256]{3,2,1,0:T(8,128)(2,1)S(1)}, u32[]{:S(2)}, u32[]{:S(2)}) async-start(bf16[32,6,16,256]{3,2,1,0:T(8,128)(2,1)} %copy-done.8), calls=%async_computation.1 | async-start | bytes 3145728 | tf_op jit(solution)/shard_map/all_to_all | solution.py:276
  46.3 37.5 %collective-permute-start = (bf16[2048,1024]{1,0:T(8,128)(2,1)}, bf16[2048,1024]{1,0:T(8,128)(2,1)}, u32[]{:S(2)}, u32[]{:S(2)}) collective-permute-start(bf16[2048,1024]{1,0:T(8,128)(2,1)} %copy-done.7), channel_id=1, source_target_pairs={{0,32},{32,0},{64,96},{96,64},{1,33},{33,1},{65,97},{97,65},{2,34}... | collective-permute-start | bytes 12582920 | tf_op jit(solution)/shard_map/ppermute | solution.py:275
  70.9 1.2 copy-start.2
  70.9 12.9 %copy-start.1 = (bf16[2048,1024]{1,0:T(8,128)(2,1)S(1)}, bf16[2048,1024]{1,0:T(8,128)(2,1)}, u32[]{:S(2)}) copy-start(bf16[2048,1024]{1,0:T(8,128)(2,1)} %get-tuple-element.34.mine_ref) | copy-start | bytes 12582916
  74.0 45.9 %collective-permute-start.7 = (bf16[2048,1024]{1,0:T(8,128)(2,1)}, bf16[2048,1024]{1,0:T(8,128)(2,1)S(1)}, u32[]{:S(2)}, u32[]{:S(2)}) collective-permute-start(bf16[2048,1024]{1,0:T(8,128)(2,1)} %get-tuple-element.48), channel_id=1, source_target_pairs={{0,32},{32,0},{64,96},{96,64},{1,33},{33,1},{65,97},{97,65},{2,34}... | collective-permute-start | bytes 12582920 | tf_op jit(solution)/shard_map/ppermute | solution.py:281
  74.5 9.2 %collective-permute-start.1 = (bf16[32,6,16,256]{3,2,1,0:T(8,128)(2,1)}, bf16[32,6,16,256]{3,2,1,0:T(8,128)(2,1)S(1)}, u32[]{:S(2)}, u32[]{:S(2)}) collective-permute-start(bf16[32,6,16,256]{3,2,1,0:T(8,128)(2,1)} %get-tuple-element.36.tm_ref), channel_id=1, source_target_pairs={{0,32},{32,0},{64,96},{96,64},{1,33},{33,1},{65,97},{97,65},{2,34}... | collective-permute-start | bytes 4718600 | tf_op jit(solution)/shard_map/ppermute | solution.py:279
  83.8 1.4 copy-start.3
  88.7 14.8 %collective-permute-start.2 = (bf16[1024,256]{1,0:T(8,128)(2,1)S(1)}, bf16[1024,256]{1,0:T(8,128)(2,1)S(1)}, u32[]{:S(2)}, u32[]{:S(2)}) collective-permute-start(bf16[1024,256]{1,0:T(8,128)(2,1)S(1)} %get-tuple-element.40), channel_id=1, source_target_pairs={{0,64},{32,96},{64,0},{96,32},{1,65},{33,97},{65,1},{97,33},{2,66}... | collective-permute-start | bytes 1572872 | tf_op jit(solution)/shard_map/ppermute | solution.py:289
  93.3 21.4 %collective-permute-start.3 = (bf16[1024,256]{1,0:T(8,128)(2,1)S(1)}, bf16[1024,256]{1,0:T(8,128)(2,1)S(1)}, u32[]{:S(2)}, u32[]{:S(2)}) collective-permute-start(bf16[1024,256]{1,0:T(8,128)(2,1)S(1)} %get-tuple-element.42), channel_id=1, source_target_pairs={{0,64},{32,96},{64,0},{96,32},{1,65},{33,97},{65,1},{97,33},{2,66}... | collective-permute-start | bytes 1572872 | tf_op jit(solution)/shard_map/ppermute | solution.py:289
  99.9 37.3 %collective-permute-start.6 = (bf16[2048,256]{1,0:T(8,128)(2,1)S(1)}, bf16[2048,256]{1,0:T(8,128)(2,1)S(1)}, u32[]{:S(2)}, u32[]{:S(2)}) collective-permute-start(bf16[2048,256]{1,0:T(8,128)(2,1)S(1)} %get-tuple-element.45), channel_id=1, source_target_pairs={{0,64},{32,96},{64,0},{96,32},{1,65},{33,97},{65,1},{97,33},{2,66}... | collective-permute-start | bytes 3145736 | tf_op jit(solution)/shard_map/ppermute | solution.py:289
  107.1 41.4 %collective-permute-start.5 = (bf16[1024,256]{1,0:T(8,128)(2,1)S(1)}, bf16[1024,256]{1,0:T(8,128)(2,1)S(1)}, u32[]{:S(2)}, u32[]{:S(2)}) collective-permute-start(bf16[1024,256]{1,0:T(8,128)(2,1)S(1)} %get-tuple-element.44), channel_id=1, source_target_pairs={{0,64},{32,96},{64,0},{96,32},{1,65},{33,97},{65,1},{97,33},{2,66}... | collective-permute-start | bytes 1572872 | tf_op jit(solution)/shard_map/ppermute | solution.py:289
  114.8 5.2 %copy-start.4 = (bf16[32,6,16,256]{3,2,1,0:T(8,128)(2,1)S(1)}, bf16[32,6,16,256]{3,2,1,0:T(8,128)(2,1)}, u32[]{:S(2)}) copy-start(bf16[32,6,16,256]{3,2,1,0:T(8,128)(2,1)} %get-tuple-element.36.tm_ref) | copy-start | bytes 4718596
  114.8 5.2 %copy-start.5 = (bf16[2048,1024]{1,0:T(8,128)(2,1)S(1)}, bf16[2048,1024]{1,0:T(8,128)(2,1)}, u32[]{:S(2)}) copy-start(bf16[2048,1024]{1,0:T(8,128)(2,1)} %get-tuple-element.47.mine_ref) | copy-start | bytes 12582916
  118.8 40.3 %collective-permute-start.4 = (bf16[1024,256]{1,0:T(8,128)(2,1)S(1)}, bf16[1024,256]{1,0:T(8,128)(2,1)S(1)}, u32[]{:S(2)}, u32[]{:S(2)}) collective-permute-start(bf16[1024,256]{1,0:T(8,128)(2,1)S(1)} %get-tuple-element.43), channel_id=1, source_target_pairs={{0,64},{32,96},{64,0},{96,32},{1,65},{33,97},{65,1},{97,33},{2,66}... | collective-permute-start | bytes 1572872 | tf_op jit(solution)/shard_map/ppermute | solution.py:289

commit v3 on v2

--- a/solution.py
+++ b/solution.py
@@ -14,6 +14,7 @@
 PIECES = 8
 TB = 128
 CUTS = 4
+AHEAD = 4
 MIB = 1024 * 1024
 VMEM = pl.BlockSpec(memory_space=pltpu.VMEM)
 SMEM = pl.BlockSpec(memory_space=pltpu.SMEM)
@@ -32,10 +33,11 @@
     )
 
 
-def gather_body(parts, q_ref, ids_ref, codes_ref, sc_ref, *rest):
+def gather_body(parts, after, q_ref, ids_ref, codes_ref, sc_ref, *rest):
     n = len(parts)
-    outs, token = rest[:n], rest[n]
-    wide, held, stage, sem_in, sem_out = rest[n + 1 :]
+    rest = rest[after:]
+    outs, token = rest[: 2 * n], rest[2 * n]
+    wide, held, stage, sem_in, sem_out = rest[2 * n + 1 :]
     rows, width = held.shape
     nb = width // LANES
     piece = rows // PIECES
@@ -68,15 +70,16 @@
             )
     q = q_ref[0]
     token[0] = q
-    for p, x in enumerate(parts):
-        src = (q ^ x) * quarter
+    size = quarter // 2
+    for p in range(2 * n):
+        src = (q ^ parts[p // 2]) * quarter + p % 2 * size
 
         def block(t, carry, p=p, src=src):
             o = pl.multiple_of(t * TB, TB)
             for r in range(TB):
                 e = ids_ref[src + o + r]
                 stage[r * nb : (r + 1) * nb, :] = wide[pl.ds(pl.multiple_of(e * nb, nb), nb), :]
-            d = pl.multiple_of(p * quarter + o, TB)
+            d = pl.multiple_of(p * size + o, TB)
             for b in range(nb):
                 held[pl.ds(d, TB), b * LANES : (b + 1) * LANES] = stage[
                     pl.ds(b, TB, stride=nb), :
@@ -86,76 +89,79 @@
             ).start()
             return carry
 
-        lax.fori_loop(0, quarter // TB, block, 0)
-    for p in range(n):
-        pltpu.make_async_copy(
-            held.at[pl.ds(p * quarter, quarter)], outs[p], sem_out.at[p]
-        ).wait()
-
-
-def gather(parts, q, ids, codes, scales_t):
+        lax.fori_loop(0, size // TB, block, 0)
+    for p in range(2 * n):
+        pltpu.make_async_copy(held.at[pl.ds(p * size, size)], outs[p], sem_out.at[p]).wait()
+
+
+def gather(parts, q, ids, codes, scales_t, after=()):
     rows, width = codes.shape
     nb = scales_t.shape[0]
     n = len(parts)
     return pl.pallas_call(
-        functools.partial(gather_body, parts),
+        functools.partial(gather_body, parts, len(after)),
         grid_spec=grid_of(
             2,
             (),
-            [ANY, VMEM],
-            [ANY] * n + [SMEM],
+            [ANY, VMEM] + [ANY] * len(after),
+            [ANY] * (2 * n) + [SMEM],
             [
                 pltpu.VMEM((rows * nb, LANES), F32),
                 pltpu.VMEM((rows, width), BF),
                 pltpu.VMEM((TB * nb, LANES), F32),
                 pltpu.SemaphoreType.DMA((PIECES,)),
-                pltpu.SemaphoreType.DMA((n,)),
+                pltpu.SemaphoreType.DMA((2 * n,)),
             ],
         ),
-        out_shape=[jax.ShapeDtypeStruct((rows // 4, width), BF)] * n + [TOKEN],
+        out_shape=[jax.ShapeDtypeStruct((rows // 8, width), BF)] * (2 * n) + [TOKEN],
         compiler_params=params(54),
         name="gather_features",
-    )(q, ids, codes, scales_t)
-
-
-def pick_body(owners_ref, q_ref, rec_ref, held_ref, out_ref, token, held_out):
+    )(q, ids, codes, scales_t, *after)
+
+
+def pick_body(owners_ref, q_ref, rec_ref, out_ref, token, held, sem):
     token[0] = q_ref[0]
     n, rounds = out_ref.shape[:2]
     for r in range(rounds):
-        piece = rec_ref[owners_ref[r]]
-        for d in range(n):
-            out_ref[d, r] = piece
-
-
-def pick(owners, q, rec, held):
+        held[r] = rec_ref[owners_ref[r]]
+    copies = [pltpu.make_async_copy(held, out_ref.at[d], sem.at[d]) for d in range(n)]
+    for copy in copies:
+        copy.start()
+    for copy in copies:
+        copy.wait()
+
+
+def pick(owners, q, rec):
     n, h, w = rec.shape
+    rounds = owners.shape[0]
     return pl.pallas_call(
         pick_body,
-        grid_spec=grid_of(2, (), [VMEM, ANY], [VMEM, SMEM, ANY]),
-        out_shape=[
-            jax.ShapeDtypeStruct((n, owners.shape[0], h, w), BF),
-            TOKEN,
-            jax.ShapeDtypeStruct(held.shape, held.dtype),
-        ],
-        input_output_aliases={3: 2},
+        grid_spec=grid_of(
+            2,
+            (),
+            [VMEM],
+            [pl.BlockSpec(memory_space=pltpu.HBM), SMEM],
+            [pltpu.VMEM((rounds, h, w), BF), pltpu.SemaphoreType.DMA((n,))],
+        ),
+        out_shape=[pltpu.HBM((n, rounds, h, w), BF), TOKEN],
         compiler_params=params(8),
         name="pick_pieces",
-    )(owners, q, rec, held)
-
-
-def tie_body(q_ref, x_ref, y_ref, x_out, y_out, token):
-    token[0] = q_ref[0]
-
-
-def tie(q, x, y):
+    )(owners, q, rec)
+
+
+def tie_body(*refs):
+    pass
+
+
+def tie(q, x, after=()):
     return pl.pallas_call(
         tie_body,
-        grid_spec=grid_of(1, (), [ANY, ANY], [ANY, ANY, SMEM]),
-        out_shape=[jax.ShapeDtypeStruct(a.shape, a.dtype) for a in (x, y)] + [TOKEN],
-        input_output_aliases={1: 0, 2: 1},
-        compiler_params=params(56),
+        grid_spec=grid_of(1, (), [ANY] * (1 + len(after)), ANY),
+        out_shape=jax.ShapeDtypeStruct(x.shape, x.dtype),
+        input_output_aliases={1: 0},
+        compiler_params=params(1),
         name="tie",
-    )(q, x, y)
+    )(q, x, *after)
 
 
 def lay(raw_ref, t_ref):
@@ -184,10 +190,10 @@
     out_ref[...] = dots(mine_ref, other_ref, tm, to).astype(BF)
 
 
-def send_scores(q, mine, other, raw_m, raw_o, pair, per, start, count, after=(), block=512):
-    width = mine.shape[1]
+def send_scores(q, mine, other, raw_m, raw_o, pair, per, after=(), block=512):
+    count, width = mine.shape
     n, _, h, w = raw_m.shape
-    feats = pl.BlockSpec((block, width), lambda i, *_: (i + start // block, 0))
+    feats = pl.BlockSpec((block, width), lambda i, *_: (i, 0))
     targets = pl.BlockSpec((n, 2, h, w), lambda i, *_: (0, pair, 0, 0))
     return pl.pallas_call(
         send_body,
@@ -204,7 +210,10 @@
     )(q, mine, other, raw_m, raw_o, *after)
 
 
-def near_body(scale, q_ref, mine_ref, other_ref, tm_ref, to_ref, out_ref, tm, to):
+def near_body(scale, q_ref, mine_ref, other_ref, tm_ref, to_ref, *rest):
+    out_ref, token, tm, to = rest[-4:]
+    token[0] = q_ref[0]
+
     @pl.when(pl.program_id(0) == 0)
     def _():
         lay(tm_ref, tm)
@@ -213,24 +222,26 @@
     out_ref[...] = dots(mine_ref, other_ref, tm, to) * scale
 
 
-def near_scores(q, scale, mine, other, raw_m, raw_o, per, block=256):
+def near_scores(q, scale, mine, other, raw_m, raw_o, per, half, out, block=256):
     rows, width = mine.shape
     total = per * raw_m.shape[1]
     feats = pl.BlockSpec((block, width), lambda i, *_: (i, 0))
     raw = pl.BlockSpec(raw_m.shape, lambda i, *_: (0, 0, 0, 0))
+    given = [] if out is None else [out]
     return pl.pallas_call(
         functools.partial(near_body, scale),
         grid_spec=grid_of(
             1,
             (rows // block,),
-            [feats, feats, raw, raw],
-            pl.BlockSpec((block, total), lambda i, *_: (i, 0)),
+            [feats, feats, raw, raw] + [ANY] * len(given),
+            [pl.BlockSpec((block, total), lambda i, *_: (i + half * (rows // block), 0)), SMEM],
             [pltpu.VMEM((total, width), BF)] * 2,
         ),
-        out_shape=jax.ShapeDtypeStruct((rows, total), F32),
+        out_shape=[jax.ShapeDtypeStruct((2 * rows, total), F32), TOKEN],
+        input_output_aliases={5: 0} if given else {},
         compiler_params=params(32),
         name="near_scores",
-    )(q, mine, other, raw_m, raw_o)
+    )(q, mine, other, raw_m, raw_o, *given)
 
 
 def add_body(scale, got_ref, old_ref, out_ref):
@@ -269,36 +280,41 @@
     own = lax.dynamic_slice_in_dim(targets, q * width, width, 1)
     pieces = own.reshape(n_wide // CUTS, h, CUTS, w).transpose(0, 2, 1, 3).reshape(n_wide, h, w)
     rec = lax.all_to_all(pieces, "wide", 0, 0, tiled=True)
-    to_far, tok = gather((3,), q1, ids, codes, scales_t)
-
-    picked, tok, to_far = pick(owners, tok, rec, to_far)
-    other_far = lax.ppermute(to_far, "ckpt", other_core)
+    picked, tok = pick(owners, q1, rec)
     raw_m = lax.all_to_all(picked, "wide", 0, 0, tiled=True)
-    mine_far, to_near, mine_near, tok = gather((2, 1, 0), tok, ids, codes, scales_t)
-    raw_m, to_near, tok = tie(tok, raw_m, to_near)
+
+    *feats, tok = gather((3, 2), tok, ids, codes, scales_t)
+    mine_far = feats[2:]
+    other_far = [lax.ppermute(x, "ckpt", other_core) for x in feats[:2]]
+    raw_m = tie(tok, raw_m)
     raw_o = lax.ppermute(raw_m, "ckpt", other_core)
 
-    other_near = lax.ppermute(to_near, "ckpt", other_core)
-
-    sent = []
-    for pair, start, count in plan(owners.shape[0] // 2, quarter):
-        after = [sent[-3][0]] if len(sent) > 2 else []
+    pairs = owners.shape[0] // 2
+    steps = [(pair, half) for pair in range(pairs) for half in range(2)]
+    got = []
+    for i, (pair, half) in enumerate(steps):
+        if i == AHEAD:
+            *feats, tok = gather((1, 0), tok, ids, codes, scales_t, got[:1])
+        after = [got[i - 3]] if i >= AHEAD else []
         part, tok = send_scores(
-            tok, mine_far, other_far, raw_m, raw_o, pair, per, start, count, after
+            tok, mine_far[half], other_far[half], raw_m, raw_o, pair, per, after
         )
-        sent.append((lax.ppermute(part, "ckpt", other_chip), pair, start))
-
-    out = near_scores(tok, scale, mine_near, other_near, raw_m, raw_o, per)
-    for got, pair, start in sent:
-        out = add_scores(scale, got, out, pair, start)
+        got.append(lax.ppermute(part, "ckpt", other_chip))
+        if i == AHEAD:
+            other_near = [
+                lax.ppermute(tie(tok, x, got[2 + side : 3 + side]), "ckpt", other_core)
+                for side, x in enumerate(feats[:2])
+            ]
+    mine_near = feats[2:]
+
+    out = None
+    for half in range(2):
+        out, tok = near_scores(
+            tok, scale, mine_near[half], other_near[half], raw_m, raw_o, per, half, out
+        )
+    for (pair, half), part in zip(steps, got, strict=True):
+        out = add_scores(scale, part, out, pair, half * (quarter // 2))
     return out[None]
-
-
-def plan(pairs, rows):
-    for pair in range(pairs):
-        cuts = 2 if pair in (0, pairs - 1) else 1
-        for c in range(cuts):
-            yield pair, c * (rows // cuts), rows // cuts
 
 
 def solution(mesh):

time: 163 us -> 143 us (0.88)
  waiting for transfers between devices: 37.4 us -> 12.5 us
  blocking collectives: 0 us -> 21 us
  starting transfers between devices: 27.2 us -> 11.4 us
  local copies, waits for them, and re-layouts: 10.1 us -> 2.26 us
  Pallas kernels: 86.3 us -> 93.8 us
    ppermute x7 -> x10, waiting for transfers between devices: 28.3 us -> 6.92 us  [the longest x6 5.2 us: per_device(): got.append(lax.ppermute(part, 'ckpt', other_chip))]
    all_to_all x0 -> x1, blocking collectives: none -> 21 us  [per_device(): rec = lax.all_to_all(pieces, 'wide', 0, 0, tiled=True)]
    all_to_all x1 -> x0, starting transfers between devices: 10.7 us -> none  [per_device(): rec = lax.all_to_all(pieces, 'wide', 0, 0, tiled=True)]
    unnamed x20, local copies, waits for them, and re-layouts: 9.2 us -> 2.04 us
    all_to_all x1, starting transfers between devices: 9.83 us -> 4.05 us  [per_device(): raw_m = lax.all_to_all(picked, 'wide', 0, 0, tiled=True)]
    ppermute x1, waiting for transfers between devices: 9.15 us -> 4.16 us  [per_device(): raw_o = lax.ppermute(raw_m, 'ckpt', other_core)]
    pallas_call x5 -> x6, Pallas kernels: 20 us -> 23.3 us  [send_scores(): pl.pallas_call(send_body, grid_spec=grid_of(1, (count // block,), [feats,...]
    pallas_call x1 -> x2, Pallas kernels: 9.86 us -> 12 us  [near_scores(): pl.pallas_call(functools.partial(near_body, scale), grid_spec=grid_of(1,...]
  transfers between devices with their start and end apart: 10 -> 12, of which waited for: 6 -> 4; matrix products, arithmetic and copies ran while one was open for 0% -> 0% of each run, Pallas kernels for 51% -> 63%
where the time goes in v3:
time: 143 us; the launch traced here: 141 us
  Pallas kernels  93.8 us (66%)
  blocking collectives  21 us (15%)
  waiting for transfers between devices  12.5 us (9%)
  starting transfers between devices  11.4 us (8%)
  local copies, waits for them, and re-layouts  2.26 us (2%)
    pallas_call x2, Pallas kernels, gather(): pl.pallas_call(functools.partial(gather_body, parts, len(after)), grid_sp...  41.3 us
    pallas_call x6, Pallas kernels, send_scores(): pl.pallas_call(send_body, grid_spec=grid_of(1, (count // block,), [feats,...  23.3 us
    all_to_all x1, blocking collectives, per_device(): rec = lax.all_to_all(pieces, 'wide', 0, 0, tiled=True)  21 us
    pallas_call x6, Pallas kernels, add_scores(): pl.pallas_call(functools.partial(add_body, scale), grid=(count // block,)...  12.5 us
    pallas_call x2, Pallas kernels, near_scores(): pl.pallas_call(functools.partial(near_body, scale), grid_spec=grid_of(1,...  12 us
    ppermute x6, starting transfers between devices, per_device(): got.append(lax.ppermute(part, 'ckpt', other_chip))  6.55 us
    ppermute x6, waiting for transfers between devices, per_device(): got.append(lax.ppermute(part, 'ckpt', other_chip))  5.2 us
    ppermute x1, waiting for transfers between devices, per_device(): raw_o = lax.ppermute(raw_m, 'ckpt', other_core)  4.16 us
  transfers between devices with their start and end apart: 12, of which 4 were waited for; matrix products, arithmetic and copies ran while one was open for 0% of the time, Pallas kernels for 63%

profile of v3, /device:TPU:0, one launch (start us, length us, event | category | flops | bytes accessed | tf_op | source)
XLA Modules:
  0.0 141.2 jit_solution(10685145070018561422)
XLA Ops:
  1.5 21.0 %all_to_all.10.rec_ref = bf16[32,16,256]{2,1,0:T(8,128)(2,1)S(1)} all-to-all(bf16[32,16,256]{2,1,0:T(8,128)(2,1)S(1)} %bitcast.14), channel_id=1, replica_groups=mesh['ckpt'=4,'wide'=32] {'wide'}, dimensions={0} | all-to-all | bytes 524288 | tf_op jit(solution)/shard_map/all_to_all | solution.py:282
  22.5 2.5 %pick_pieces.1 = (bf16[32,6,16,256]{3,2,1,0:T(8,128)(2,1)}, s32[1]{0:T(128)}) custom-call(s32[6]{0:T(128)S(1)} %copy-done.9, s32[1]{0:T(128)} %bitcast.q_ref, bf16[32,16,256]{2,1,0:T(8,128)(2,1)S(1)} %all_to_all.10.rec_ref), custom_call_target="tpu_custom_call" | custom-call | tf_op jit(solution)/shard_map/pick_pieces/pallas_call | solution.py:137
  25.0 4.0 %all-to-all-start.1 = ((bf16[32,6,16,256]{3,2,1,0:T(8,128)(2,1)}), bf16[32,6,16,256]{3,2,1,0:T(8,128)(2,1)S(1)}, u32[]{:S(2)}, u32[]{:S(2)}) async-start(bf16[32,6,16,256]{3,2,1,0:T(8,128)(2,1)} %get-tuple-element.36), calls=%async_computation.1 | async-start | bytes 3145728 | tf_op jit(solution)/shard_map/all_to_all | solution.py:284
  29.0 20.7 %gather_features.2 = (bf16[1024,1024]{1,0:T(8,128)(2,1)}, bf16[1024,1024]{1,0:T(8,128)(2,1)}, bf16[1024,1024]{1,0:T(8,128)(2,1)}, bf16[1024,1024]{1,0:T(8,128)(2,1)}, s32[1]{0:T(128)}) custom-call(s32[1]{0:T(128)} %get-tuple-element.32.q_ref, s32[8192]{0:T(1024)} %bitcast.15, bf16[8192,1024]{1,0:T(8,128)(2,1)} %bitcast.9, f32[8,8192]{1,0:T(8,128)} %bitcast.11), custom_call_target="tpu_custom_call" | custom-call | tf_op jit(solution)/shard_map/gather_features/pallas_call | solution.py:101
  50.3 1.4 all-to-all-done.1.refs_1_
  52.6 1.7 %collective-permute-done.other_ref = bf16[1024,1024]{1,0:T(8,128)(2,1)} collective-permute-done((bf16[1024,1024]{1,0:T(8,128)(2,1)}, bf16[1024,1024]{1,0:T(8,128)(2,1)}, u32[]{:S(2)}, u32[]{:S(2)}) %collective-permute-start) | collective-permute-done | bytes 2097184 | tf_op jit(solution)/shard_map/ppermute | solution.py:288
  54.3 4.2 %collective-permute-done.1.to_ref = bf16[32,6,16,256]{3,2,1,0:T(8,128)(2,1)S(1)} collective-permute-done((bf16[32,6,16,256]{3,2,1,0:T(8,128)(2,1)S(1)}, bf16[32,6,16,256]{3,2,1,0:T(8,128)(2,1)S(1)}, u32[]{:S(2)}, u32[]{:S(2)}) %collective-permute-start.1) | collective-permute-done | bytes 1572896 | tf_op jit(solution)/shard_map/ppermute | solution.py:290
  58.5 3.6 %send_scores.6 = (bf16[1024,256]{1,0:T(8,128)(2,1)S(1)}, s32[1]{0:T(128)}) custom-call(s32[1]{0:T(128)} %get-tuple-element.33.refs_0_.q_ref, bf16[1024,1024]{1,0:T(8,128)(2,1)S(1)} %copy-done.2, bf16[1024,1024]{1,0:T(8,128)(2,1)} %collective-permute-done.other_ref, bf16[32,6,16,256]{3,2,1,0:T(8,128)(2,1)S(1)} %tie.3.tm_ref, ...), custom_call_target="tpu_custom_call" | custom-call | tf_op jit(solution)/shard_map/send_scores/pallas_call | solution.py:198
  63.2 4.2 %send_scores.7 = (bf16[1024,256]{1,0:T(8,128)(2,1)}, s32[1]{0:T(128)}) custom-call(s32[1]{0:T(128)} %get-tuple-element.37.q_ref, bf16[1024,1024]{1,0:T(8,128)(2,1)S(1)} %copy-done.1, bf16[1024,1024]{1,0:T(8,128)(2,1)} %collective-permute-done.2.other_ref, bf16[32,6,16,256]{3,2,1,0:T(8,128)(2,1)S(1)} %tie.3.tm_ref, ...), custom_call_target="tpu_custom_call" | custom-call | tf_op jit(solution)/shard_map/send_scores/pallas_call | solution.py:198
  68.4 4.2 %send_scores.8 = (bf16[1024,256]{1,0:T(8,128)(2,1)}, s32[1]{0:T(128)}) custom-call(s32[1]{0:T(128)} %get-tuple-element.40.q_ref, bf16[1024,1024]{1,0:T(8,128)(2,1)S(1)} %copy-done.2, bf16[1024,1024]{1,0:T(8,128)(2,1)} %collective-permute-done.other_ref, bf16[32,6,16,256]{3,2,1,0:T(8,128)(2,1)S(1)} %tie.3.tm_ref, ...), custom_call_target="tpu_custom_call" | custom-call | tf_op jit(solution)/shard_map/send_scores/pallas_call | solution.py:198
  73.6 4.2 %send_scores.9 = (bf16[1024,256]{1,0:T(8,128)(2,1)}, s32[1]{0:T(128)}) custom-call(s32[1]{0:T(128)} %get-tuple-element.41.q_ref, bf16[1024,1024]{1,0:T(8,128)(2,1)S(1)} %copy-done.1, bf16[1024,1024]{1,0:T(8,128)(2,1)} %collective-permute-done.2.other_ref, bf16[32,6,16,256]{3,2,1,0:T(8,128)(2,1)S(1)} %tie.3.tm_ref, ...), custom_call_target="tpu_custom_call" | custom-call | tf_op jit(solution)/shard_map/send_scores/pallas_call | solution.py:198
  79.6 20.6 %gather_features.3 = (bf16[1024,1024]{1,0:T(8,128)(2,1)}, bf16[1024,1024]{1,0:T(8,128)(2,1)}, bf16[1024,1024]{1,0:T(8,128)(2,1)}, bf16[1024,1024]{1,0:T(8,128)(2,1)}, s32[1]{0:T(128)}) custom-call(s32[1]{0:T(128)} %get-tuple-element.42.q_ref, s32[8192]{0:T(1024)} %bitcast.16, bf16[8192,1024]{1,0:T(8,128)(2,1)} %bitcast.10, f32[8,8192]{1,0:T(8,128)} %bitcast.12, ...), custom_call_target="tpu_custom_call" | custom-call | tf_op jit(solution)/shard_map/gather_features/pallas_call | solution.py:101
  100.3 3.6 %send_scores.10 = (bf16[1024,256]{1,0:T(8,128)(2,1)S(1)}, s32[1]{0:T(128)}) custom-call(s32[1]{0:T(128)} %get-tuple-element.44.q_ref, bf16[1024,1024]{1,0:T(8,128)(2,1)S(1)} %copy-done.2, bf16[1024,1024]{1,0:T(8,128)(2,1)} %collective-permute-done.other_ref, bf16[32,6,16,256]{3,2,1,0:T(8,128)(2,1)S(1)} %tie.3.tm_ref, ...), custom_call_target="tpu_custom_call" | custom-call | tf_op jit(solution)/shard_map/send_scores/pallas_call | solution.py:198
  104.8 5.2 %collective-permute-done.8.refs_2_.got_ref = bf16[1024,256]{1,0:T(8,128)(2,1)} collective-permute-done((bf16[1024,256]{1,0:T(8,128)(2,1)}, bf16[1024,256]{1,0:T(8,128)(2,1)}, u32[]{:S(2)}, u32[]{:S(2)}) %collective-permute-start.8) | collective-permute-done | bytes 524320 | tf_op jit(solution)/shard_map/ppermute | solution.py:302
  110.7 1.3 collective-permute-start.7
  112.0 3.5 %send_scores.11 = (bf16[1024,256]{1,0:T(8,128)(2,1)S(1)}, s32[1]{0:T(128)}) custom-call(s32[1]{0:T(128)} %get-tuple-element.46.q_ref.refs_0_, bf16[1024,1024]{1,0:T(8,128)(2,1)S(1)} %copy-done.1, bf16[1024,1024]{1,0:T(8,128)(2,1)} %collective-permute-done.2.other_ref, bf16[32,6,16,256]{3,2,1,0:T(8,128)(2,1)S(1)} %tie.3.tm_ref, ...), custom_call_target="tpu_custom_call" | custom-call | tf_op jit(solution)/shard_map/send_scores/pallas_call | solution.py:198
  116.6 6.1 %near_scores.2 = (f32[2048,768]{1,0:T(8,128)}, s32[1]{0:T(128)}) custom-call(s32[1]{0:T(128)} %get-tuple-element.51.q_ref, bf16[1024,1024]{1,0:T(8,128)(2,1)S(1)} %copy-done.8, bf16[1024,1024]{1,0:T(8,128)(2,1)S(1)} %collective-permute-done.9.other_ref, bf16[32,6,16,256]{3,2,1,0:T(8,128)(2,1)S(1)} %tie.3.tm_ref, ...), custom_call_target="tpu_custom_call" | custom-call | tf_op jit(solution)/shard_map/near_scores/pallas_call | solution.py:231
  122.7 5.9 %near_scores.3 = (f32[2048,768]{1,0:T(8,128)}, s32[1]{0:T(128)}) custom-call(s32[1]{0:T(128)} %get-tuple-element.54.q_ref, bf16[1024,1024]{1,0:T(8,128)(2,1)S(1)} %copy-done.7, bf16[1024,1024]{1,0:T(8,128)(2,1)S(1)} %collective-permute-done.10.other_ref, bf16[32,6,16,256]{3,2,1,0:T(8,128)(2,1)S(1)} %tie.3.tm_ref, ...), custom_call_target="tpu_custom_call", output_to_operand_aliasing={{0}: (5, {})} | custom-call | tf_op jit(solution)/shard_map/near_scores/pallas_call | solution.py:231
  128.7 2.1 %add_scores.6.old_ref = f32[2048,768]{1,0:T(8,128)} custom-call(bf16[1024,256]{1,0:T(8,128)(2,1)S(1)} %copy-done.4, f32[2048,768]{1,0:T(8,128)} %get-tuple-element.58.old_ref), custom_call_target="tpu_custom_call", output_to_operand_aliasing={{}: (1, {})} | custom-call | tf_op jit(solution)/shard_map/add_scores/pallas_call | solution.py:254
  130.8 2.1 %add_scores.7.old_ref = f32[2048,768]{1,0:T(8,128)} custom-call(bf16[1024,256]{1,0:T(8,128)(2,1)S(1)} %collective-permute-done.4.rest_0_.got_ref, f32[2048,768]{1,0:T(8,128)} %add_scores.6.old_ref), custom_call_target="tpu_custom_call", output_to_operand_aliasing={{}: (1, {})} | custom-call | tf_op jit(solution)/shard_map/add_scores/pallas_call | solution.py:254
  132.8 2.1 %add_scores.8.old_ref = f32[2048,768]{1,0:T(8,128)} custom-call(bf16[1024,256]{1,0:T(8,128)(2,1)S(1)} %collective-permute-done.5.rest_0_.refs_2_.got_ref, f32[2048,768]{1,0:T(8,128)} %add_scores.7.old_ref), custom_call_target="tpu_custom_call", output_to_operand_aliasing={{}: (1, {})} | custom-call | tf_op jit(solution)/shard_map/add_scores/pallas_call | solution.py:254
  134.9 2.2 %add_scores.9.old_ref = f32[2048,768]{1,0:T(8,128)} custom-call(bf16[1024,256]{1,0:T(8,128)(2,1)} %collective-permute-done.8.refs_2_.got_ref, f32[2048,768]{1,0:T(8,128)} %add_scores.8.old_ref), custom_call_target="tpu_custom_call", output_to_operand_aliasing={{}: (1, {})} | custom-call | tf_op jit(solution)/shard_map/add_scores/pallas_call | solution.py:254
  137.1 2.1 %add_scores.10.old_ref = f32[2048,768]{1,0:T(8,128)} custom-call(bf16[1024,256]{1,0:T(8,128)(2,1)S(1)} %collective-permute-done.7.got_ref, f32[2048,768]{1,0:T(8,128)} %add_scores.9.old_ref), custom_call_target="tpu_custom_call", output_to_operand_aliasing={{}: (1, {})} | custom-call | tf_op jit(solution)/shard_map/add_scores/pallas_call | solution.py:254
  139.2 2.1 %add_scores.11 = f32[2048,768]{1,0:T(8,128)} custom-call(bf16[1024,256]{1,0:T(8,128)(2,1)S(1)} %collective-permute-done.6.got_ref, f32[2048,768]{1,0:T(8,128)} %add_scores.10.old_ref), custom_call_target="tpu_custom_call", output_to_operand_aliasing={{}: (1, {})} | custom-call | tf_op jit(solution)/shard_map/add_scores/pallas_call | solution.py:254
  (44 shorter events, 10.5 us)
Async XLA Ops:
  0.0 1.2 copy-start
  0.0 22.5 %copy-start.9 = (s32[6]{0:T(128)S(1)}, s32[6]{0:T(128)}, u32[]{:S(2)}) copy-start(s32[6]{0:T(128)} %owners_ref.1) | copy-start | bytes 76
  25.0 26.8 %all-to-all-start.1 = ((bf16[32,6,16,256]{3,2,1,0:T(8,128)(2,1)}), bf16[32,6,16,256]{3,2,1,0:T(8,128)(2,1)S(1)}, u32[]{:S(2)}, u32[]{:S(2)}) async-start(bf16[32,6,16,256]{3,2,1,0:T(8,128)(2,1)} %get-tuple-element.36), calls=%async_computation.1 | async-start | bytes 3145728 | tf_op jit(solution)/shard_map/all_to_all | solution.py:284
  49.7 4.6 %collective-permute-start = (bf16[1024,1024]{1,0:T(8,128)(2,1)}, bf16[1024,1024]{1,0:T(8,128)(2,1)}, u32[]{:S(2)}, u32[]{:S(2)}) collective-permute-start(bf16[1024,1024]{1,0:T(8,128)(2,1)} %get-tuple-element.35), channel_id=1, source_target_pairs={{0,32},{32,0},{64,96},{96,64},{1,33},{33,1},{65,97},{97,65},{2,34}... | collective-permute-start | bytes 6291464 | tf_op jit(solution)/shard_map/ppermute | solution.py:288
  49.8 13.4 %collective-permute-start.2 = (bf16[1024,1024]{1,0:T(8,128)(2,1)}, bf16[1024,1024]{1,0:T(8,128)(2,1)}, u32[]{:S(2)}, u32[]{:S(2)}) collective-permute-start(bf16[1024,1024]{1,0:T(8,128)(2,1)} %get-tuple-element.39), channel_id=1, source_target_pairs={{0,32},{32,0},{64,96},{96,64},{1,33},{33,1},{65,97},{97,65},{2,34}... | collective-permute-start | bytes 6291464 | tf_op jit(solution)/shard_map/ppermute | solution.py:288
  51.7 6.7 %copy-start.2 = (bf16[1024,1024]{1,0:T(8,128)(2,1)S(1)}, bf16[1024,1024]{1,0:T(8,128)(2,1)}, u32[]{:S(2)}) copy-start(bf16[1024,1024]{1,0:T(8,128)(2,1)} %get-tuple-element.34.mine_ref) | copy-start | bytes 6291460
  52.5 6.0 %collective-permute-start.1 = (bf16[32,6,16,256]{3,2,1,0:T(8,128)(2,1)S(1)}, bf16[32,6,16,256]{3,2,1,0:T(8,128)(2,1)S(1)}, u32[]{:S(2)}, u32[]{:S(2)}) collective-permute-start(bf16[32,6,16,256]{3,2,1,0:T(8,128)(2,1)S(1)} %tie.3.tm_ref), channel_id=1, source_target_pairs={{0,32},{32,0},{64,96},{96,64},{1,33},{33,1},{65,97},{97,65},{2,34}... | collective-permute-start | bytes 4718600 | tf_op jit(solution)/shard_map/ppermute | solution.py:290
  58.5 4.8 %copy-start.1 = (bf16[1024,1024]{1,0:T(8,128)(2,1)S(1)}, bf16[1024,1024]{1,0:T(8,128)(2,1)}, u32[]{:S(2)}) copy-start(bf16[1024,1024]{1,0:T(8,128)(2,1)} %get-tuple-element.38.mine_ref) | copy-start | bytes 6291460
  62.1 16.7 %collective-permute-start.3 = (bf16[1024,256]{1,0:T(8,128)(2,1)S(1)}, bf16[1024,256]{1,0:T(8,128)(2,1)S(1)}, u32[]{:S(2)}, u32[]{:S(2)}) collective-permute-start(bf16[1024,256]{1,0:T(8,128)(2,1)S(1)} %get-tuple-element.43), channel_id=1, source_target_pairs={{0,64},{32,96},{64,0},{96,32},{1,65},{33,97},{65,1},{97,33},{2,66}... | collective-permute-start | bytes 1572872 | tf_op jit(solution)/shard_map/ppermute | solution.py:302
  67.4 32.8 %collective-permute-start.4 = (bf16[1024,256]{1,0:T(8,128)(2,1)}, bf16[1024,256]{1,0:T(8,128)(2,1)S(1)}, u32[]{:S(2)}, u32[]{:S(2)}) collective-permute-start(bf16[1024,256]{1,0:T(8,128)(2,1)} %get-tuple-element.45), channel_id=1, source_target_pairs={{0,64},{32,96},{64,0},{96,32},{1,65},{33,97},{65,1},{97,33},{2,66}... | collective-permute-start | bytes 1572872 | tf_op jit(solution)/shard_map/ppermute | solution.py:302
  72.6 31.3 %collective-permute-start.5 = (bf16[1024,256]{1,0:T(8,128)(2,1)}, bf16[1024,256]{1,0:T(8,128)(2,1)S(1)}, u32[]{:S(2)}, u32[]{:S(2)}) collective-permute-start(bf16[1024,256]{1,0:T(8,128)(2,1)} %get-tuple-element.47), channel_id=1, source_target_pairs={{0,64},{32,96},{64,0},{96,32},{1,65},{33,97},{65,1},{97,33},{2,66}... | collective-permute-start | bytes 1572872 | tf_op jit(solution)/shard_map/ppermute | solution.py:302
  77.8 32.2 %collective-permute-start.8 = (bf16[1024,256]{1,0:T(8,128)(2,1)}, bf16[1024,256]{1,0:T(8,128)(2,1)}, u32[]{:S(2)}, u32[]{:S(2)}) collective-permute-start(bf16[1024,256]{1,0:T(8,128)(2,1)} %get-tuple-element.50), channel_id=1, source_target_pairs={{0,64},{32,96},{64,0},{96,32},{1,65},{33,97},{65,1},{97,33},{2,66}... | collective-permute-start | bytes 1572872 | tf_op jit(solution)/shard_map/ppermute | solution.py:302
  78.8 0.8 copy-start.3
  100.2 3.7 %copy-start.6 = (bf16[1024,1024]{1,0:T(8,128)(2,1)S(1)}, bf16[1024,1024]{1,0:T(8,128)(2,1)}, u32[]{:S(2)}) copy-start(bf16[1024,1024]{1,0:T(8,128)(2,1)} %get-tuple-element.53.refs_1_) | copy-start | bytes 6291460
  103.9 6.1 %copy-start.5 = (bf16[1024,1024]{1,0:T(8,128)(2,1)S(1)}, bf16[1024,1024]{1,0:T(8,128)(2,1)}, u32[]{:S(2)}) copy-start(bf16[1024,1024]{1,0:T(8,128)(2,1)} %get-tuple-element.56.refs_1_) | copy-start | bytes 6291460
  104.7 11.9 %collective-permute-start.9 = (bf16[1024,1024]{1,0:T(8,128)(2,1)S(1)}, bf16[1024,1024]{1,0:T(8,128)(2,1)S(1)}, u32[]{:S(2)}, u32[]{:S(2)}) collective-permute-start(bf16[1024,1024]{1,0:T(8,128)(2,1)S(1)} %tie.4), channel_id=1, source_target_pairs={{0,32},{32,0},{64,96},{96,64},{1,33},{33,1},{65,97},{97,65},{2,34}... | collective-permute-start | bytes 6291464 | tf_op jit(solution)/shard_map/ppermute | solution.py:305
  110.6 12.1 %collective-permute-start.10 = (bf16[1024,1024]{1,0:T(8,128)(2,1)S(1)}, bf16[1024,1024]{1,0:T(8,128)(2,1)S(1)}, u32[]{:S(2)}, u32[]{:S(2)}) collective-permute-start(bf16[1024,1024]{1,0:T(8,128)(2,1)S(1)} %tie.5), channel_id=1, source_target_pairs={{0,32},{32,0},{64,96},{96,64},{1,33},{33,1},{65,97},{97,65},{2,34}... | collective-permute-start | bytes 6291464 | tf_op jit(solution)/shard_map/ppermute | solution.py:305
  110.7 5.9 %copy-start.8 = (bf16[1024,1024]{1,0:T(8,128)(2,1)S(1)}, bf16[1024,1024]{1,0:T(8,128)(2,1)}, u32[]{:S(2)}) copy-start(bf16[1024,1024]{1,0:T(8,128)(2,1)} %get-tuple-element.52.mine_ref) | copy-start | bytes 6291460
  110.7 26.4 %collective-permute-start.7 = (bf16[1024,256]{1,0:T(8,128)(2,1)S(1)}, bf16[1024,256]{1,0:T(8,128)(2,1)S(1)}, u32[]{:S(2)}, u32[]{:S(2)}) collective-permute-start(bf16[1024,256]{1,0:T(8,128)(2,1)S(1)} %get-tuple-element.49), channel_id=1, source_target_pairs={{0,64},{32,96},{64,0},{96,32},{1,65},{33,97},{65,1},{97,33},{2,66}... | collective-permute-start | bytes 1572872 | tf_op jit(solution)/shard_map/ppermute | solution.py:302
  115.5 23.6 %collective-permute-start.6 = (bf16[1024,256]{1,0:T(8,128)(2,1)S(1)}, bf16[1024,256]{1,0:T(8,128)(2,1)S(1)}, u32[]{:S(2)}, u32[]{:S(2)}) collective-permute-start(bf16[1024,256]{1,0:T(8,128)(2,1)S(1)} %get-tuple-element.48), channel_id=1, source_target_pairs={{0,64},{32,96},{64,0},{96,32},{1,65},{33,97},{65,1},{97,33},{2,66}... | collective-permute-start | bytes 1572872 | tf_op jit(solution)/shard_map/ppermute | solution.py:302
  116.6 6.1 %copy-start.7 = (bf16[1024,1024]{1,0:T(8,128)(2,1)S(1)}, bf16[1024,1024]{1,0:T(8,128)(2,1)}, u32[]{:S(2)}) copy-start(bf16[1024,1024]{1,0:T(8,128)(2,1)} %get-tuple-element.55.mine_ref) | copy-start | bytes 6291460
  122.7 5.9 %copy-start.4 = (bf16[1024,256]{1,0:T(8,128)(2,1)S(1)}, bf16[1024,256]{1,0:T(8,128)(2,1)}, u32[]{:S(2)}) copy-start(bf16[1024,256]{1,0:T(8,128)(2,1)} %copy-done.3) | copy-start | bytes 1572868

commit v4 on v3

--- a/solution.py
+++ b/solution.py
@@ -121,10 +121,15 @@
 
 def pick_body(owners_ref, q_ref, rec_ref, out_ref, token, held, sem):
     token[0] = q_ref[0]
-    n, rounds = out_ref.shape[:2]
+    m, rounds = held.shape[:2]
+    n = out_ref.shape[0] // m
     for r in range(rounds):
-        held[r] = rec_ref[owners_ref[r]]
-    copies = [pltpu.make_async_copy(held, out_ref.at[d], sem.at[d]) for d in range(n)]
+        piece = rec_ref[owners_ref[r]]
+        for i in range(m):
+            held[i, r] = piece
+    copies = [
+        pltpu.make_async_copy(held, out_ref.at[pl.ds(d * m, m)], sem.at[d]) for d in range(n)
+    ]
     for copy in copies:
         copy.start()
     for copy in copies:
@@ -141,7 +146,7 @@
             (),
             [VMEM],
             [pl.BlockSpec(memory_space=pltpu.HBM), SMEM],
-            [pltpu.VMEM((rounds, h, w), BF), pltpu.SemaphoreType.DMA((n,))],
+            [pltpu.VMEM((CUTS, rounds, h, w), BF), pltpu.SemaphoreType.DMA((n // CUTS,))],
         ),
         out_shape=[pltpu.HBM((n, rounds, h, w), BF), TOKEN],
         compiler_params=params(8),
@@ -210,7 +215,7 @@
     )(q, mine, other, raw_m, raw_o, *after)
 
 
-def near_body(scale, q_ref, mine_ref, other_ref, tm_ref, to_ref, *rest):
+def near_body(scale, parts, q_ref, mine_ref, other_ref, tm_ref, to_ref, *rest):
     out_ref, token, tm, to = rest[-4:]
     token[0] = q_ref[0]
 
@@ -219,29 +224,35 @@
         lay(tm_ref, tm)
         lay(to_ref, to)
 
-    out_ref[...] = dots(mine_ref, other_ref, tm, to) * scale
-
-
-def near_scores(q, scale, mine, other, raw_m, raw_o, per, half, out, block=256):
+    acc = dots(mine_ref, other_ref, tm, to)
+    cols = 0
+    for part in rest[:parts]:
+        first, cols = cols, cols + part.shape[1]
+        out_ref[:, first:cols] = (acc[:, first:cols] + part[...].astype(F32)) * scale
+    out_ref[:, cols:] = acc[:, cols:] * scale
+
+
+def near_scores(q, scale, mine, other, raw_m, raw_o, per, half, parts, out, block=256):
     rows, width = mine.shape
     total = per * raw_m.shape[1]
     feats = pl.BlockSpec((block, width), lambda i, *_: (i, 0))
     raw = pl.BlockSpec(raw_m.shape, lambda i, *_: (0, 0, 0, 0))
     given = [] if out is None else [out]
-    return pl.pallas_call(
-        functools.partial(near_body, scale),
+    cells = [pl.BlockSpec((block, p.shape[1]), lambda i, *_: (i, 0)) for p in parts]
+    return pl.pallas_call(
+        functools.partial(near_body, scale, len(parts)),
         grid_spec=grid_of(
             1,
             (rows // block,),
-            [feats, feats, raw, raw] + [ANY] * len(given),
+            [feats, feats, raw, raw] + cells + [ANY] * len(given),
             [pl.BlockSpec((block, total), lambda i, *_: (i + half * (rows // block), 0)), SMEM],
             [pltpu.VMEM((total, width), BF)] * 2,
         ),
         out_shape=[jax.ShapeDtypeStruct((2 * rows, total), F32), TOKEN],
-        input_output_aliases={5: 0} if given else {},
+        input_output_aliases={5 + len(parts): 0} if given else {},
         compiler_params=params(32),
         name="near_scores",
-    )(q, mine, other, raw_m, raw_o, *given)
+    )(q, mine, other, raw_m, raw_o, *parts, *given)
 
 
 def add_body(scale, got_ref, old_ref, out_ref):
@@ -284,8 +295,8 @@
     raw_m = lax.all_to_all(picked, "wide", 0, 0, tiled=True)
 
     *feats, tok = gather((3, 2), tok, ids, codes, scales_t)
-    mine_far = feats[2:]
-    other_far = [lax.ppermute(x, "ckpt", other_core) for x in feats[:2]]
+    mine_far, to_far = feats[2:], feats[1]
+    other_far = [lax.ppermute(feats[0], "ckpt", other_core)]
     raw_m = tie(tok, raw_m)
     raw_o = lax.ppermute(raw_m, "ckpt", other_core)
 
@@ -300,6 +311,8 @@
             tok, mine_far[half], other_far[half], raw_m, raw_o, pair, per, after
         )
         got.append(lax.ppermute(part, "ckpt", other_chip))
+        if i == 0:
+            other_far.append(lax.ppermute(tie(tok, to_far), "ckpt", other_core))
         if i == AHEAD:
             other_near = [
                 lax.ppermute(tie(tok, x, got[2 + side : 3 + side]), "ckpt", other_core)
@@ -310,9 +323,9 @@
     out = None
     for half in range(2):
         out, tok = near_scores(
-            tok, scale, mine_near[half], other_near[half], raw_m, raw_o, per, half, out
+            tok, scale, mine_near[half], other_near[half], raw_m, raw_o, per, half, got[half:-2:2], out
         )
-    for (pair, half), part in zip(steps, got, strict=True):
+    for (pair, half), part in list(zip(steps, got, strict=True))[-2:]:
         out = add_scores(scale, part, out, pair, half * (quarter // 2))
     return out[None]
 

time: 143 us -> 138 us (0.965)
  Pallas kernels: 93.8 us -> 83.6 us
  waiting for transfers between devices: 12.5 us -> 19 us
    pallas_call x6 -> x2, Pallas kernels: 12.5 us -> 4.13 us  [add_scores(): pl.pallas_call(functools.partial(add_body, scale), grid=(count // block,)...]
    ppermute x6, waiting for transfers between devices: 5.2 us -> 10.4 us  [per_device(): got.append(lax.ppermute(part, 'ckpt', other_chip))]
    pallas_call x6, Pallas kernels: 23.3 us -> 19.9 us  [send_scores(): pl.pallas_call(send_body, grid_spec=grid_of(1, (count // block,), [feats,...]
    ppermute x2, waiting for transfers between devices: 1.71 us -> 4.82 us  [the longest x1 3 us: per_device(): other_far.append(lax.ppermute(tie(tok, to_far), 'ckpt', other_core))]
    ppermute x1, waiting for transfers between devices: 4.16 us -> 1.91 us  [per_device(): raw_o = lax.ppermute(raw_m, 'ckpt', other_core)]
    pallas_call x3 -> x4, Pallas kernels: 2.15 us -> 3.05 us  [tie(): pl.pallas_call(tie_body, grid_spec=grid_of(1, (), [ANY] * (1 + len(after)...]
  transfers between devices with their start and end apart: 12 -> 12, of which waited for: 4 -> 6; matrix products, arithmetic and copies ran while one was open for 0% -> 0% of each run, Pallas kernels for 63% -> 55%
where the time goes in v4:
time: 138 us; the launch traced here: 137 us
  Pallas kernels  83.6 us (61%)
  blocking collectives  21 us (15%)
  waiting for transfers between devices  19 us (14%)
  starting transfers between devices  11.1 us (8%)
  local copies, waits for them, and re-layouts  2.28 us (2%)
    pallas_call x2, Pallas kernels, gather(): pl.pallas_call(functools.partial(gather_body, parts, len(after)), grid_sp...  41.5 us
    all_to_all x1, blocking collectives, per_device(): rec = lax.all_to_all(pieces, 'wide', 0, 0, tiled=True)  21 us
    pallas_call x6, Pallas kernels, send_scores(): pl.pallas_call(send_body, grid_spec=grid_of(1, (count // block,), [feats,...  19.9 us
    pallas_call x2, Pallas kernels, near_scores(): pl.pallas_call(functools.partial(near_body, scale, len(parts)), grid_spec...  12.8 us
    ppermute x6, waiting for transfers between devices, per_device(): got.append(lax.ppermute(part, 'ckpt', other_chip))  10.4 us
    ppermute x6, starting transfers between devices, per_device(): got.append(lax.ppermute(part, 'ckpt', other_chip))  6.47 us
    pallas_call x2, Pallas kernels, add_scores(): pl.pallas_call(functools.partial(add_body, scale), grid=(count // block,)...  4.13 us
    all_to_all x1, starting transfers between devices, per_device(): raw_m = lax.all_to_all(picked, 'wide', 0, 0, tiled=True)  4.05 us
  transfers between devices with their start and end apart: 12, of which 6 were waited for; matrix products, arithmetic and copies ran while one was open for 0% of the time, Pallas kernels for 55%

profile of v4, /device:TPU:0, one launch (start us, length us, event | category | flops | bytes accessed | tf_op | source)
XLA Modules:
  0.0 137.3 jit_solution(10184881059801986631)
XLA Ops:
  0.0 1.2 copy-done
  1.5 21.0 %all_to_all.10.rec_ref = bf16[32,16,256]{2,1,0:T(8,128)(2,1)S(1)} all-to-all(bf16[32,16,256]{2,1,0:T(8,128)(2,1)S(1)} %bitcast.14), channel_id=1, replica_groups=mesh['ckpt'=4,'wide'=32] {'wide'}, dimensions={0} | all-to-all | bytes 524288 | tf_op jit(solution)/shard_map/all_to_all | solution.py:293
  22.5 2.3 %pick_pieces.1 = (bf16[32,6,16,256]{3,2,1,0:T(8,128)(2,1)}, s32[1]{0:T(128)}) custom-call(s32[6]{0:T(128)S(1)} %copy-done.12, s32[1]{0:T(128)} %bitcast.q_ref, bf16[32,16,256]{2,1,0:T(8,128)(2,1)S(1)} %all_to_all.10.rec_ref), custom_call_target="tpu_custom_call" | custom-call | tf_op jit(solution)/shard_map/pick_pieces/pallas_call | solution.py:142
  24.8 4.0 %all-to-all-start.1 = ((bf16[32,6,16,256]{3,2,1,0:T(8,128)(2,1)}), bf16[32,6,16,256]{3,2,1,0:T(8,128)(2,1)S(1)}, u32[]{:S(2)}, u32[]{:S(2)}) async-start(bf16[32,6,16,256]{3,2,1,0:T(8,128)(2,1)} %get-tuple-element.36), calls=%async_computation.1 | async-start | bytes 3145728 | tf_op jit(solution)/shard_map/all_to_all | solution.py:295
  28.8 20.8 %gather_features.2 = (bf16[1024,1024]{1,0:T(8,128)(2,1)}, bf16[1024,1024]{1,0:T(8,128)(2,1)}, bf16[1024,1024]{1,0:T(8,128)(2,1)}, bf16[1024,1024]{1,0:T(8,128)(2,1)}, s32[1]{0:T(128)}) custom-call(s32[1]{0:T(128)} %get-tuple-element.32.q_ref, s32[8192]{0:T(1024)} %bitcast.15, bf16[8192,1024]{1,0:T(8,128)(2,1)} %bitcast.9, f32[8,8192]{1,0:T(8,128)} %bitcast.11), custom_call_target="tpu_custom_call" | custom-call | tf_op jit(solution)/shard_map/gather_features/pallas_call | solution.py:101
  49.7 1.8 %all-to-all-done.1.refs_1_ = bf16[32,6,16,256]{3,2,1,0:T(8,128)(2,1)S(1)} async-done(((bf16[32,6,16,256]{3,2,1,0:T(8,128)(2,1)}), bf16[32,6,16,256]{3,2,1,0:T(8,128)(2,1)S(1)}, u32[]{:S(2)}, u32[]{:S(2)}) %all-to-all-start.1) | async-done | bytes 1572896 | tf_op jit(solution)/shard_map/all_to_all | solution.py:295
  52.4 1.8 %collective-permute-done.other_ref = bf16[1024,1024]{1,0:T(8,128)(2,1)} collective-permute-done((bf16[1024,1024]{1,0:T(8,128)(2,1)}, bf16[1024,1024]{1,0:T(8,128)(2,1)}, u32[]{:S(2)}, u32[]{:S(2)}) %collective-permute-start) | collective-permute-done | bytes 2097184 | tf_op jit(solution)/shard_map/ppermute | solution.py:299
  54.2 1.9 %collective-permute-done.1.to_ref = bf16[32,6,16,256]{3,2,1,0:T(8,128)(2,1)S(1)} collective-permute-done((bf16[32,6,16,256]{3,2,1,0:T(8,128)(2,1)S(1)}, bf16[32,6,16,256]{3,2,1,0:T(8,128)(2,1)S(1)}, u32[]{:S(2)}, u32[]{:S(2)}) %collective-permute-start.1) | collective-permute-done | bytes 1572896 | tf_op jit(solution)/shard_map/ppermute | solution.py:301
  56.1 3.6 %send_scores.6 = (bf16[1024,256]{1,0:T(8,128)(2,1)S(1)}, s32[1]{0:T(128)}) custom-call(s32[1]{0:T(128)} %get-tuple-element.33.refs_0_.q_ref, bf16[1024,1024]{1,0:T(8,128)(2,1)S(1)} %copy-done.2, bf16[1024,1024]{1,0:T(8,128)(2,1)} %collective-permute-done.other_ref, bf16[32,6,16,256]{3,2,1,0:T(8,128)(2,1)S(1)} %tie.4.tm_ref, ...), custom_call_target="tpu_custom_call" | custom-call | tf_op jit(solution)/shard_map/send_scores/pallas_call | solution.py:203
  61.8 3.0 %collective-permute-done.2.other_ref = bf16[1024,1024]{1,0:T(8,128)(2,1)S(1)} collective-permute-done((bf16[1024,1024]{1,0:T(8,128)(2,1)S(1)}, bf16[1024,1024]{1,0:T(8,128)(2,1)S(1)}, u32[]{:S(2)}, u32[]{:S(2)}) %collective-permute-start.2) | collective-permute-done | bytes 2097184 | tf_op jit(solution)/shard_map/ppermute | solution.py:315
  64.8 3.1 %send_scores.7 = (bf16[1024,256]{1,0:T(8,128)(2,1)}, s32[1]{0:T(128)}) custom-call(s32[1]{0:T(128)} %get-tuple-element.37.refs_0_.q_ref, bf16[1024,1024]{1,0:T(8,128)(2,1)S(1)} %copy-done.1, bf16[1024,1024]{1,0:T(8,128)(2,1)S(1)} %collective-permute-done.2.other_ref, bf16[32,6,16,256]{3,2,1,0:T(8,128)(2,1)S(1)} %tie.4.tm_ref, ...), custom_call_target="tpu_custom_call" | custom-call | tf_op jit(solution)/shard_map/send_scores/pallas_call | solution.py:203
  68.9 4.2 %send_scores.8 = (bf16[1024,256]{1,0:T(8,128)(2,1)}, s32[1]{0:T(128)}) custom-call(s32[1]{0:T(128)} %get-tuple-element.40.q_ref, bf16[1024,1024]{1,0:T(8,128)(2,1)S(1)} %copy-done.2, bf16[1024,1024]{1,0:T(8,128)(2,1)} %collective-permute-done.other_ref, bf16[32,6,16,256]{3,2,1,0:T(8,128)(2,1)S(1)} %tie.4.tm_ref, ...), custom_call_target="tpu_custom_call" | custom-call | tf_op jit(solution)/shard_map/send_scores/pallas_call | solution.py:203
  74.0 3.1 %send_scores.9 = (bf16[1024,256]{1,0:T(8,128)(2,1)}, s32[1]{0:T(128)}) custom-call(s32[1]{0:T(128)} %get-tuple-element.41.q_ref, bf16[1024,1024]{1,0:T(8,128)(2,1)S(1)} %copy-done.1, bf16[1024,1024]{1,0:T(8,128)(2,1)S(1)} %collective-permute-done.2.other_ref, bf16[32,6,16,256]{3,2,1,0:T(8,128)(2,1)S(1)} %tie.4.tm_ref, ...), custom_call_target="tpu_custom_call" | custom-call | tf_op jit(solution)/shard_map/send_scores/pallas_call | solution.py:203
  78.9 20.8 %gather_features.3 = (bf16[1024,1024]{1,0:T(8,128)(2,1)}, bf16[1024,1024]{1,0:T(8,128)(2,1)}, bf16[1024,1024]{1,0:T(8,128)(2,1)}, bf16[1024,1024]{1,0:T(8,128)(2,1)}, s32[1]{0:T(128)}) custom-call(s32[1]{0:T(128)} %get-tuple-element.42.q_ref, s32[8192]{0:T(1024)} %bitcast.16, bf16[8192,1024]{1,0:T(8,128)(2,1)} %bitcast.10, f32[8,8192]{1,0:T(8,128)} %bitcast.12, ...), custom_call_target="tpu_custom_call" | custom-call | tf_op jit(solution)/shard_map/gather_features/pallas_call | solution.py:101
  99.7 3.6 %send_scores.10 = (bf16[1024,256]{1,0:T(8,128)(2,1)S(1)}, s32[1]{0:T(128)}) custom-call(s32[1]{0:T(128)} %get-tuple-element.44.q_ref, bf16[1024,1024]{1,0:T(8,128)(2,1)S(1)} %copy-done.2, bf16[1024,1024]{1,0:T(8,128)(2,1)} %collective-permute-done.other_ref, bf16[32,6,16,256]{3,2,1,0:T(8,128)(2,1)S(1)} %tie.4.tm_ref, ...), custom_call_target="tpu_custom_call" | custom-call | tf_op jit(solution)/shard_map/send_scores/pallas_call | solution.py:203
  104.2 4.5 %collective-permute-done.9.refs_2_.rest_1_ = bf16[1024,256]{1,0:T(8,128)(2,1)} collective-permute-done((bf16[1024,256]{1,0:T(8,128)(2,1)}, bf16[1024,256]{1,0:T(8,128)(2,1)}, u32[]{:S(2)}, u32[]{:S(2)}) %collective-permute-start.9) | collective-permute-done | bytes 524320 | tf_op jit(solution)/shard_map/ppermute | solution.py:313
  109.7 1.3 collective-permute-start.7
  111.0 2.3 %send_scores.11 = (bf16[1024,256]{1,0:T(8,128)(2,1)S(1)}, s32[1]{0:T(128)}) custom-call(s32[1]{0:T(128)} %get-tuple-element.46.q_ref.refs_0_, bf16[1024,1024]{1,0:T(8,128)(2,1)S(1)} %copy-done.1, bf16[1024,1024]{1,0:T(8,128)(2,1)S(1)} %copy-done.4, bf16[32,6,16,256]{3,2,1,0:T(8,128)(2,1)S(1)} %tie.4.tm_ref, ...), custom_call_target="tpu_custom_call" | custom-call | tf_op jit(solution)/shard_map/send_scores/pallas_call | solution.py:203
  113.3 1.1 collective-permute-start.6
  114.4 6.1 %near_scores.2 = (f32[2048,768]{1,0:T(8,128)}, s32[1]{0:T(128)}) custom-call(s32[1]{0:T(128)} %get-tuple-element.50.q_ref, bf16[1024,1024]{1,0:T(8,128)(2,1)S(1)} %copy-done.11, bf16[1024,1024]{1,0:T(8,128)(2,1)S(1)} %collective-permute-done.8.other_ref, bf16[32,6,16,256]{3,2,1,0:T(8,128)(2,1)S(1)} %tie.4.tm_ref, ...), custom_call_target="tpu_custom_call" | custom-call | tf_op jit(solution)/shard_map/near_scores/pallas_call | solution.py:242
  120.5 6.7 %near_scores.3 = (f32[2048,768]{1,0:T(8,128)}, s32[1]{0:T(128)}) custom-call(s32[1]{0:T(128)} %get-tuple-element.53.q_ref, bf16[1024,1024]{1,0:T(8,128)(2,1)S(1)} %copy-done.10, bf16[1024,1024]{1,0:T(8,128)(2,1)S(1)} %collective-permute-done.10.other_ref, bf16[32,6,16,256]{3,2,1,0:T(8,128)(2,1)S(1)} %tie.4.tm_ref, ...), custom_call_target="tpu_custom_call", output_to_operand_aliasing={{0}: (7, {})} | custom-call | tf_op jit(solution)/shard_map/near_scores/pallas_call | solution.py:242
  127.2 2.1 %add_scores.2.old_ref = f32[2048,768]{1,0:T(8,128)} custom-call(bf16[1024,256]{1,0:T(8,128)(2,1)S(1)} %collective-permute-done.7.got_ref, f32[2048,768]{1,0:T(8,128)} %get-tuple-element.58.old_ref), custom_call_target="tpu_custom_call", output_to_operand_aliasing={{}: (1, {})} | custom-call | tf_op jit(solution)/shard_map/add_scores/pallas_call | solution.py:265
  129.3 5.9 %collective-permute-done.6.got_ref = bf16[1024,256]{1,0:T(8,128)(2,1)S(1)} collective-permute-done((bf16[1024,256]{1,0:T(8,128)(2,1)S(1)}, bf16[1024,256]{1,0:T(8,128)(2,1)S(1)}, u32[]{:S(2)}, u32[]{:S(2)}) %collective-permute-start.6) | collective-permute-done | bytes 524320 | tf_op jit(solution)/shard_map/ppermute | solution.py:313
  135.2 2.1 %add_scores.3 = f32[2048,768]{1,0:T(8,128)} custom-call(bf16[1024,256]{1,0:T(8,128)(2,1)S(1)} %collective-permute-done.6.got_ref, f32[2048,768]{1,0:T(8,128)} %add_scores.2.old_ref), custom_call_target="tpu_custom_call", output_to_operand_aliasing={{}: (1, {})} | custom-call | tf_op jit(solution)/shard_map/add_scores/pallas_call | solution.py:265
  (47 shorter events, 8.7 us)
Async XLA Ops:
  0.0 1.2 copy-start
  0.0 22.5 %copy-start.12 = (s32[6]{0:T(128)S(1)}, s32[6]{0:T(128)}, u32[]{:S(2)}) copy-start(s32[6]{0:T(128)} %owners_ref.1) | copy-start | bytes 76
  24.8 26.8 %all-to-all-start.1 = ((bf16[32,6,16,256]{3,2,1,0:T(8,128)(2,1)}), bf16[32,6,16,256]{3,2,1,0:T(8,128)(2,1)S(1)}, u32[]{:S(2)}, u32[]{:S(2)}) async-start(bf16[32,6,16,256]{3,2,1,0:T(8,128)(2,1)} %get-tuple-element.36), calls=%async_computation.1 | async-start | bytes 3145728 | tf_op jit(solution)/shard_map/all_to_all | solution.py:295
  49.6 4.6 %collective-permute-start = (bf16[1024,1024]{1,0:T(8,128)(2,1)}, bf16[1024,1024]{1,0:T(8,128)(2,1)}, u32[]{:S(2)}, u32[]{:S(2)}) collective-permute-start(bf16[1024,1024]{1,0:T(8,128)(2,1)} %get-tuple-element.35), channel_id=1, source_target_pairs={{0,32},{32,0},{64,96},{96,64},{1,33},{33,1},{65,97},{97,65},{2,34}... | collective-permute-start | bytes 6291464 | tf_op jit(solution)/shard_map/ppermute | solution.py:299
  51.6 4.5 %copy-start.2 = (bf16[1024,1024]{1,0:T(8,128)(2,1)S(1)}, bf16[1024,1024]{1,0:T(8,128)(2,1)}, u32[]{:S(2)}) copy-start(bf16[1024,1024]{1,0:T(8,128)(2,1)} %get-tuple-element.34.mine_ref) | copy-start | bytes 6291460
  52.3 3.8 %collective-permute-start.1 = (bf16[32,6,16,256]{3,2,1,0:T(8,128)(2,1)S(1)}, bf16[32,6,16,256]{3,2,1,0:T(8,128)(2,1)S(1)}, u32[]{:S(2)}, u32[]{:S(2)}) collective-permute-start(bf16[32,6,16,256]{3,2,1,0:T(8,128)(2,1)S(1)} %tie.4.tm_ref), channel_id=1, source_target_pairs={{0,32},{32,0},{64,96},{96,64},{1,33},{33,1},{65,97},{97,65},{2,34}... | collective-permute-start | bytes 4718600 | tf_op jit(solution)/shard_map/ppermute | solution.py:301
  56.1 3.6 %copy-start.9 = (bf16[1024,1024]{1,0:T(8,128)(2,1)S(1)}, bf16[1024,1024]{1,0:T(8,128)(2,1)}, u32[]{:S(2)}) copy-start(bf16[1024,1024]{1,0:T(8,128)(2,1)} %get-tuple-element.39.refs_1_) | copy-start | bytes 6291460
  59.7 5.1 %copy-start.1 = (bf16[1024,1024]{1,0:T(8,128)(2,1)S(1)}, bf16[1024,1024]{1,0:T(8,128)(2,1)}, u32[]{:S(2)}) copy-start(bf16[1024,1024]{1,0:T(8,128)(2,1)} %get-tuple-element.38.mine_ref) | copy-start | bytes 6291460
  60.5 4.2 %collective-permute-start.2 = (bf16[1024,1024]{1,0:T(8,128)(2,1)S(1)}, bf16[1024,1024]{1,0:T(8,128)(2,1)S(1)}, u32[]{:S(2)}, u32[]{:S(2)}) collective-permute-start(bf16[1024,1024]{1,0:T(8,128)(2,1)S(1)} %tie.5), channel_id=1, source_target_pairs={{0,32},{32,0},{64,96},{96,64},{1,33},{33,1},{65,97},{97,65},{2,34}... | collective-permute-start | bytes 6291464 | tf_op jit(solution)/shard_map/ppermute | solution.py:315
  60.7 17.4 %collective-permute-start.3 = (bf16[1024,256]{1,0:T(8,128)(2,1)S(1)}, bf16[1024,256]{1,0:T(8,128)(2,1)S(1)}, u32[]{:S(2)}, u32[]{:S(2)}) collective-permute-start(bf16[1024,256]{1,0:T(8,128)(2,1)S(1)} %get-tuple-element.43), channel_id=1, source_target_pairs={{0,64},{32,96},{64,0},{96,32},{1,65},{33,97},{65,1},{97,33},{2,66}... | collective-permute-start | bytes 1572872 | tf_op jit(solution)/shard_map/ppermute | solution.py:313
  64.8 9.3 %copy-start.3 = (bf16[1024,1024]{1,0:T(8,128)(2,1)}, bf16[1024,1024]{1,0:T(8,128)(2,1)S(1)}, u32[]{:S(2)}) copy-start(bf16[1024,1024]{1,0:T(8,128)(2,1)S(1)} %collective-permute-done.2.other_ref) | copy-start | bytes 6291460
  67.8 31.8 %collective-permute-start.4 = (bf16[1024,256]{1,0:T(8,128)(2,1)}, bf16[1024,256]{1,0:T(8,128)(2,1)S(1)}, u32[]{:S(2)}, u32[]{:S(2)}) collective-permute-start(bf16[1024,256]{1,0:T(8,128)(2,1)} %get-tuple-element.45), channel_id=1, source_target_pairs={{0,64},{32,96},{64,0},{96,32},{1,65},{33,97},{65,1},{97,33},{2,66}... | collective-permute-start | bytes 1572872 | tf_op jit(solution)/shard_map/ppermute | solution.py:313
  73.0 30.3 %collective-permute-start.5 = (bf16[1024,256]{1,0:T(8,128)(2,1)}, bf16[1024,256]{1,0:T(8,128)(2,1)S(1)}, u32[]{:S(2)}, u32[]{:S(2)}) collective-permute-start(bf16[1024,256]{1,0:T(8,128)(2,1)} %get-tuple-element.47), channel_id=1, source_target_pairs={{0,64},{32,96},{64,0},{96,32},{1,65},{33,97},{65,1},{97,33},{2,66}... | collective-permute-start | bytes 1572872 | tf_op jit(solution)/shard_map/ppermute | solution.py:313
  77.1 31.7 %collective-permute-start.9 = (bf16[1024,256]{1,0:T(8,128)(2,1)}, bf16[1024,256]{1,0:T(8,128)(2,1)}, u32[]{:S(2)}, u32[]{:S(2)}) collective-permute-start(bf16[1024,256]{1,0:T(8,128)(2,1)} %get-tuple-element.56), channel_id=1, source_target_pairs={{0,64},{32,96},{64,0},{96,32},{1,65},{33,97},{65,1},{97,33},{2,66}... | collective-permute-start | bytes 1572872 | tf_op jit(solution)/shard_map/ppermute | solution.py:313
  99.7 3.7 %copy-start.8 = (bf16[1024,1024]{1,0:T(8,128)(2,1)S(1)}, bf16[1024,1024]{1,0:T(8,128)(2,1)}, u32[]{:S(2)}) copy-start(bf16[1024,1024]{1,0:T(8,128)(2,1)} %get-tuple-element.52.refs_1_) | copy-start | bytes 6291460
  103.4 5.4 %copy-start.7 = (bf16[1024,1024]{1,0:T(8,128)(2,1)S(1)}, bf16[1024,1024]{1,0:T(8,128)(2,1)}, u32[]{:S(2)}) copy-start(bf16[1024,1024]{1,0:T(8,128)(2,1)} %get-tuple-element.55.refs_1_) | copy-start | bytes 6291460
  104.1 10.3 %collective-permute-start.8 = (bf16[1024,1024]{1,0:T(8,128)(2,1)S(1)}, bf16[1024,1024]{1,0:T(8,128)(2,1)S(1)}, u32[]{:S(2)}, u32[]{:S(2)}) collective-permute-start(bf16[1024,1024]{1,0:T(8,128)(2,1)S(1)} %tie.6), channel_id=1, source_target_pairs={{0,32},{32,0},{64,96},{96,64},{1,33},{33,1},{65,97},{97,65},{2,34}... | collective-permute-start | bytes 6291464 | tf_op jit(solution)/shard_map/ppermute | solution.py:318
  108.8 2.2 %copy-start.4 = (bf16[1024,1024]{1,0:T(8,128)(2,1)S(1)}, bf16[1024,1024]{1,0:T(8,128)(2,1)}, u32[]{:S(2)}) copy-start(bf16[1024,1024]{1,0:T(8,128)(2,1)} %copy-done.3) | copy-start | bytes 6291460
  109.5 10.9 %collective-permute-start.10 = (bf16[1024,1024]{1,0:T(8,128)(2,1)S(1)}, bf16[1024,1024]{1,0:T(8,128)(2,1)S(1)}, u32[]{:S(2)}, u32[]{:S(2)}) collective-permute-start(bf16[1024,1024]{1,0:T(8,128)(2,1)S(1)} %tie.7), channel_id=1, source_target_pairs={{0,32},{32,0},{64,96},{96,64},{1,33},{33,1},{65,97},{97,65},{2,34}... | collective-permute-start | bytes 6291464 | tf_op jit(solution)/shard_map/ppermute | solution.py:318
  109.6 4.8 %copy-start.6 = (bf16[1024,256]{1,0:T(8,128)(2,1)S(1)}, bf16[1024,256]{1,0:T(8,128)(2,1)}, u32[]{:S(2)}) copy-start(bf16[1024,256]{1,0:T(8,128)(2,1)} %copy-done.5) | copy-start | bytes 1572868
  109.6 4.8 %copy-start.11 = (bf16[1024,1024]{1,0:T(8,128)(2,1)S(1)}, bf16[1024,1024]{1,0:T(8,128)(2,1)}, u32[]{:S(2)}) copy-start(bf16[1024,1024]{1,0:T(8,128)(2,1)} %get-tuple-element.51.mine_ref) | copy-start | bytes 6291460
  109.7 17.6 %collective-permute-start.7 = (bf16[1024,256]{1,0:T(8,128)(2,1)S(1)}, bf16[1024,256]{1,0:T(8,128)(2,1)S(1)}, u32[]{:S(2)}, u32[]{:S(2)}) collective-permute-start(bf16[1024,256]{1,0:T(8,128)(2,1)S(1)} %get-tuple-element.49), channel_id=1, source_target_pairs={{0,64},{32,96},{64,0},{96,32},{1,65},{33,97},{65,1},{97,33},{2,66}... | collective-permute-start | bytes 1572872 | tf_op jit(solution)/shard_map/ppermute | solution.py:313
  113.3 21.9 %collective-permute-start.6 = (bf16[1024,256]{1,0:T(8,128)(2,1)S(1)}, bf16[1024,256]{1,0:T(8,128)(2,1)S(1)}, u32[]{:S(2)}, u32[]{:S(2)}) collective-permute-start(bf16[1024,256]{1,0:T(8,128)(2,1)S(1)} %get-tuple-element.48), channel_id=1, source_target_pairs={{0,64},{32,96},{64,0},{96,32},{1,65},{33,97},{65,1},{97,33},{2,66}... | collective-permute-start | bytes 1572872 | tf_op jit(solution)/shard_map/ppermute | solution.py:313
  114.4 6.1 %copy-start.10 = (bf16[1024,1024]{1,0:T(8,128)(2,1)S(1)}, bf16[1024,1024]{1,0:T(8,128)(2,1)}, u32[]{:S(2)}) copy-start(bf16[1024,1024]{1,0:T(8,128)(2,1)} %get-tuple-element.54.mine_ref) | copy-start | bytes 6291460
  (1 other events, 0.8 us)

commit v5 on v4

--- a/solution.py
+++ b/solution.py
@@ -14,7 +14,7 @@
 PIECES = 8
 TB = 128
 CUTS = 4
-AHEAD = 4
+AHEAD = 5
 MIB = 1024 * 1024
 VMEM = pl.BlockSpec(memory_space=pltpu.VMEM)
 SMEM = pl.BlockSpec(memory_space=pltpu.SMEM)
@@ -195,10 +195,10 @@
     out_ref[...] = dots(mine_ref, other_ref, tm, to).astype(BF)
 
 
-def send_scores(q, mine, other, raw_m, raw_o, pair, per, after=(), block=512):
-    count, width = mine.shape
+def send_scores(q, mine, other, raw_m, raw_o, pair, per, start, count, after=(), block=512):
+    width = mine.shape[1]
     n, _, h, w = raw_m.shape
-    feats = pl.BlockSpec((block, width), lambda i, *_: (i, 0))
+    feats = pl.BlockSpec((block, width), lambda i, *_: (i + start // block, 0))
     targets = pl.BlockSpec((n, 2, h, w), lambda i, *_: (0, pair, 0, 0))
     return pl.pallas_call(
         send_body,
@@ -300,22 +300,24 @@
     raw_m = tie(tok, raw_m)
     raw_o = lax.ppermute(raw_m, "ckpt", other_core)
 
-    pairs = owners.shape[0] // 2
-    steps = [(pair, half) for pair in range(pairs) for half in range(2)]
+    size = quarter // 2
+    head = owners.shape[0] // 2 - 1
+    steps = [(head, 0, 0, size // 2), (head, 0, size // 2, size // 2), (head, 1, 0, size)]
+    steps += [(pair, half, 0, size) for pair in range(head) for half in range(2)]
     got = []
-    for i, (pair, half) in enumerate(steps):
+    for i, (pair, half, start, count) in enumerate(steps):
         if i == AHEAD:
-            *feats, tok = gather((1, 0), tok, ids, codes, scales_t, got[:1])
-        after = [got[i - 3]] if i >= AHEAD else []
+            *feats, tok = gather((1, 0), tok, ids, codes, scales_t, got[:2])
+        after = [got[i - 3]] if i >= 3 else []
         part, tok = send_scores(
-            tok, mine_far[half], other_far[half], raw_m, raw_o, pair, per, after
+            tok, mine_far[half], other_far[half], raw_m, raw_o, pair, per, start, count, after
         )
         got.append(lax.ppermute(part, "ckpt", other_chip))
         if i == 0:
             other_far.append(lax.ppermute(tie(tok, to_far), "ckpt", other_core))
         if i == AHEAD:
             other_near = [
-                lax.ppermute(tie(tok, x, got[2 + side : 3 + side]), "ckpt", other_core)
+                lax.ppermute(tie(tok, x, got[3 + side : 4 + side]), "ckpt", other_core)
                 for side, x in enumerate(feats[:2])
             ]
     mine_near = feats[2:]
@@ -323,10 +325,11 @@
     out = None
     for half in range(2):
         out, tok = near_scores(
-            tok, scale, mine_near[half], other_near[half], raw_m, raw_o, per, half, got[half:-2:2], out
+            tok, scale, mine_near[half], other_near[half], raw_m, raw_o, per, half, got[3 + half : 4 + half], out
         )
-    for (pair, half), part in list(zip(steps, got, strict=True))[-2:]:
-        out = add_scores(scale, part, out, pair, half * (quarter // 2))
+    for i in (0, 1, 2, *range(AHEAD, len(steps))):
+        pair, half, start, _ = steps[i]
+        out = add_scores(scale, got[i], out, pair, half * size + start)
     return out[None]
 
 

time: 138 us -> 138 us (level)
  waiting for transfers between devices: 19 us -> 11 us
  Pallas kernels: 83.6 us -> 90.3 us
    pallas_call x2 -> x5, Pallas kernels: 4.13 us -> 10 us  [add_scores(): pl.pallas_call(functools.partial(add_body, scale), grid=(count // block,)...]
    ppermute x6 -> x7, waiting for transfers between devices: 10.4 us -> 5.45 us  [per_device(): got.append(lax.ppermute(part, 'ckpt', other_chip))]
    ppermute x1, waiting for transfers between devices: 3 us -> 0.01 us  [per_device(): other_far.append(lax.ppermute(tie(tok, to_far), 'ckpt', other_core))]
    pallas_call x6 -> x7, Pallas kernels: 19.9 us -> 21.6 us  [send_scores(): pl.pallas_call(send_body, grid_spec=grid_of(1, (count // block,), [feats,...]
    ppermute x6 -> x7, starting transfers between devices: 6.47 us -> 7.55 us  [per_device(): got.append(lax.ppermute(part, 'ckpt', other_chip))]
  transfers between devices with their start and end apart: 12 -> 13, of which waited for: 6 -> 7; matrix products, arithmetic and copies ran while one was open for 0% -> 0% of each run, Pallas kernels for 55% -> 60%
where the time goes in v5:
time: 138 us; the launch traced here: 136 us
  Pallas kernels  90.3 us (65%)
  blocking collectives  21 us (15%)
  starting transfers between devices  12.4 us (9%)
  waiting for transfers between devices  11 us (8%)
  local copies, waits for them, and re-layouts  1.51 us (1%)
    pallas_call x2, Pallas kernels, gather(): pl.pallas_call(functools.partial(gather_body, parts, len(after)), grid_sp...  41.4 us
    pallas_call x7, Pallas kernels, send_scores(): pl.pallas_call(send_body, grid_spec=grid_of(1, (count // block,), [feats,...  21.6 us
    all_to_all x1, blocking collectives, per_device(): rec = lax.all_to_all(pieces, 'wide', 0, 0, tiled=True)  21 us
    pallas_call x2, Pallas kernels, near_scores(): pl.pallas_call(functools.partial(near_body, scale, len(parts)), grid_spec...  11.9 us
    pallas_call x5, Pallas kernels, add_scores(): pl.pallas_call(functools.partial(add_body, scale), grid=(count // block,)...  10 us
    ppermute x7, starting transfers between devices, per_device(): got.append(lax.ppermute(part, 'ckpt', other_chip))  7.55 us
    ppermute x7, waiting for transfers between devices, per_device(): got.append(lax.ppermute(part, 'ckpt', other_chip))  5.45 us
    all_to_all x1, starting transfers between devices, per_device(): raw_m = lax.all_to_all(picked, 'wide', 0, 0, tiled=True)  4.05 us
  transfers between devices with their start and end apart: 13, of which 7 were waited for; matrix products, arithmetic and copies ran while one was open for 0% of the time, Pallas kernels for 60%

profile of v5, /device:TPU:0, one launch (start us, length us, event | category | flops | bytes accessed | tf_op | source)
XLA Modules:
  0.0 136.4 jit_solution(5274842321841761215)
XLA Ops:
  1.5 21.0 %all_to_all.10.rec_ref = bf16[32,16,256]{2,1,0:T(8,128)(2,1)S(1)} all-to-all(bf16[32,16,256]{2,1,0:T(8,128)(2,1)S(1)} %bitcast.14), channel_id=1, replica_groups=mesh['ckpt'=4,'wide'=32] {'wide'}, dimensions={0} | all-to-all | bytes 524288 | tf_op jit(solution)/shard_map/all_to_all | solution.py:293
  22.5 2.3 %pick_pieces.1 = (bf16[32,6,16,256]{3,2,1,0:T(8,128)(2,1)}, s32[1]{0:T(128)}) custom-call(s32[6]{0:T(128)S(1)} %copy-done.14, s32[1]{0:T(128)} %bitcast.q_ref, bf16[32,16,256]{2,1,0:T(8,128)(2,1)S(1)} %all_to_all.10.rec_ref), custom_call_target="tpu_custom_call" | custom-call | tf_op jit(solution)/shard_map/pick_pieces/pallas_call | solution.py:142
  24.8 4.0 %all-to-all-start.1 = ((bf16[32,6,16,256]{3,2,1,0:T(8,128)(2,1)}), bf16[32,6,16,256]{3,2,1,0:T(8,128)(2,1)S(1)}, u32[]{:S(2)}, u32[]{:S(2)}) async-start(bf16[32,6,16,256]{3,2,1,0:T(8,128)(2,1)} %get-tuple-element.38), calls=%async_computation.1 | async-start | bytes 3145728 | tf_op jit(solution)/shard_map/all_to_all | solution.py:295
  28.9 20.7 %gather_features.2 = (bf16[1024,1024]{1,0:T(8,128)(2,1)}, bf16[1024,1024]{1,0:T(8,128)(2,1)}, bf16[1024,1024]{1,0:T(8,128)(2,1)}, bf16[1024,1024]{1,0:T(8,128)(2,1)}, s32[1]{0:T(128)}) custom-call(s32[1]{0:T(128)} %get-tuple-element.34.q_ref, s32[8192]{0:T(1024)} %bitcast.15, bf16[8192,1024]{1,0:T(8,128)(2,1)} %bitcast.9, f32[8,8192]{1,0:T(8,128)} %bitcast.11), custom_call_target="tpu_custom_call" | custom-call | tf_op jit(solution)/shard_map/gather_features/pallas_call | solution.py:101
  49.6 1.9 %all-to-all-done.1.refs_1_ = bf16[32,6,16,256]{3,2,1,0:T(8,128)(2,1)S(1)} async-done(((bf16[32,6,16,256]{3,2,1,0:T(8,128)(2,1)}), bf16[32,6,16,256]{3,2,1,0:T(8,128)(2,1)S(1)}, u32[]{:S(2)}, u32[]{:S(2)}) %all-to-all-start.1) | async-done | bytes 1572896 | tf_op jit(solution)/shard_map/all_to_all | solution.py:295
  52.4 1.7 %collective-permute-done.other_ref = bf16[1024,1024]{1,0:T(8,128)(2,1)} collective-permute-done((bf16[1024,1024]{1,0:T(8,128)(2,1)}, bf16[1024,1024]{1,0:T(8,128)(2,1)}, u32[]{:S(2)}, u32[]{:S(2)}) %collective-permute-start) | collective-permute-done | bytes 2097184 | tf_op jit(solution)/shard_map/ppermute | solution.py:299
  54.1 1.9 %collective-permute-done.1.to_ref = bf16[32,6,16,256]{3,2,1,0:T(8,128)(2,1)S(1)} collective-permute-done((bf16[32,6,16,256]{3,2,1,0:T(8,128)(2,1)S(1)}, bf16[32,6,16,256]{3,2,1,0:T(8,128)(2,1)S(1)}, u32[]{:S(2)}, u32[]{:S(2)}) %collective-permute-start.1) | collective-permute-done | bytes 1572896 | tf_op jit(solution)/shard_map/ppermute | solution.py:301
  56.0 2.7 %send_scores.7 = (bf16[512,256]{1,0:T(8,128)(2,1)S(1)}, s32[1]{0:T(128)}) custom-call(s32[1]{0:T(128)} %get-tuple-element.35.refs_0_.q_ref, bf16[1024,1024]{1,0:T(8,128)(2,1)S(1)} %copy-done.1, bf16[1024,1024]{1,0:T(8,128)(2,1)} %collective-permute-done.other_ref, bf16[32,6,16,256]{3,2,1,0:T(8,128)(2,1)S(1)} %tie.4.tm_ref, ...), custom_call_target="tpu_custom_call" | custom-call | tf_op jit(solution)/shard_map/send_scores/pallas_call | solution.py:203
  60.7 2.6 %send_scores.8 = (bf16[512,256]{1,0:T(8,128)(2,1)S(1)}, s32[1]{0:T(128)}) custom-call(s32[1]{0:T(128)} %get-tuple-element.39.q_ref.refs_0_, bf16[1024,1024]{1,0:T(8,128)(2,1)S(1)} %copy-done.1, bf16[1024,1024]{1,0:T(8,128)(2,1)} %collective-permute-done.other_ref, bf16[32,6,16,256]{3,2,1,0:T(8,128)(2,1)S(1)} %tie.4.tm_ref, ...), custom_call_target="tpu_custom_call" | custom-call | tf_op jit(solution)/shard_map/send_scores/pallas_call | solution.py:203
  63.3 1.3 collective-permute-start.4
  64.6 3.0 %send_scores.9 = (bf16[1024,256]{1,0:T(8,128)(2,1)}, s32[1]{0:T(128)}) custom-call(s32[1]{0:T(128)} %get-tuple-element.40.q_ref, bf16[1024,1024]{1,0:T(8,128)(2,1)S(1)} %copy-done.2, bf16[1024,1024]{1,0:T(8,128)(2,1)S(1)} %collective-permute-done.2.other_ref, bf16[32,6,16,256]{3,2,1,0:T(8,128)(2,1)S(1)} %tie.4.tm_ref, ...), custom_call_target="tpu_custom_call" | custom-call | tf_op jit(solution)/shard_map/send_scores/pallas_call | solution.py:203
  68.8 4.2 %send_scores.10 = (bf16[1024,256]{1,0:T(8,128)(2,1)}, s32[1]{0:T(128)}) custom-call(s32[1]{0:T(128)} %get-tuple-element.43.q_ref, bf16[1024,1024]{1,0:T(8,128)(2,1)S(1)} %copy-done.1, bf16[1024,1024]{1,0:T(8,128)(2,1)} %collective-permute-done.other_ref, bf16[32,6,16,256]{3,2,1,0:T(8,128)(2,1)S(1)} %tie.4.tm_ref, ...), custom_call_target="tpu_custom_call" | custom-call | tf_op jit(solution)/shard_map/send_scores/pallas_call | solution.py:203
  74.4 3.0 %send_scores.11 = (bf16[1024,256]{1,0:T(8,128)(2,1)}, s32[1]{0:T(128)}) custom-call(s32[1]{0:T(128)} %get-tuple-element.45.q_ref, bf16[1024,1024]{1,0:T(8,128)(2,1)S(1)} %copy-done.2, bf16[1024,1024]{1,0:T(8,128)(2,1)S(1)} %collective-permute-done.2.other_ref, bf16[32,6,16,256]{3,2,1,0:T(8,128)(2,1)S(1)} %tie.4.tm_ref, ...), custom_call_target="tpu_custom_call" | custom-call | tf_op jit(solution)/shard_map/send_scores/pallas_call | solution.py:203
  78.5 20.7 %gather_features.3 = (bf16[1024,1024]{1,0:T(8,128)(2,1)}, bf16[1024,1024]{1,0:T(8,128)(2,1)}, bf16[1024,1024]{1,0:T(8,128)(2,1)}, bf16[1024,1024]{1,0:T(8,128)(2,1)}, s32[1]{0:T(128)}) custom-call(s32[1]{0:T(128)} %get-tuple-element.47.q_ref, s32[8192]{0:T(1024)} %bitcast.16, bf16[8192,1024]{1,0:T(8,128)(2,1)} %bitcast.10, f32[8,8192]{1,0:T(8,128)} %bitcast.12, ...), custom_call_target="tpu_custom_call" | custom-call | tf_op jit(solution)/shard_map/gather_features/pallas_call | solution.py:101
  99.2 3.7 %send_scores.12 = (bf16[1024,256]{1,0:T(8,128)(2,1)S(1)}, s32[1]{0:T(128)}) custom-call(s32[1]{0:T(128)} %get-tuple-element.48.q_ref, bf16[1024,1024]{1,0:T(8,128)(2,1)S(1)} %copy-done.1, bf16[1024,1024]{1,0:T(8,128)(2,1)} %collective-permute-done.other_ref, bf16[32,6,16,256]{3,2,1,0:T(8,128)(2,1)S(1)} %tie.4.tm_ref, ...), custom_call_target="tpu_custom_call" | custom-call | tf_op jit(solution)/shard_map/send_scores/pallas_call | solution.py:203
  103.8 3.8 %collective-permute-done.10.refs_2_.rest_0_ = bf16[1024,256]{1,0:T(8,128)(2,1)S(1)} collective-permute-done((bf16[1024,256]{1,0:T(8,128)(2,1)}, bf16[1024,256]{1,0:T(8,128)(2,1)S(1)}, u32[]{:S(2)}, u32[]{:S(2)}) %collective-permute-start.10) | collective-permute-done | bytes 524320 | tf_op jit(solution)/shard_map/ppermute | solution.py:315
  109.9 2.4 %send_scores.13 = (bf16[1024,256]{1,0:T(8,128)(2,1)S(1)}, s32[1]{0:T(128)}) custom-call(s32[1]{0:T(128)} %get-tuple-element.50.q_ref.refs_0_, bf16[1024,1024]{1,0:T(8,128)(2,1)S(1)} %copy-done.2, bf16[1024,1024]{1,0:T(8,128)(2,1)S(1)} %copy-done.4, bf16[32,6,16,256]{3,2,1,0:T(8,128)(2,1)S(1)} %tie.4.tm_ref, ...), custom_call_target="tpu_custom_call" | custom-call | tf_op jit(solution)/shard_map/send_scores/pallas_call | solution.py:203
  113.3 6.0 %near_scores.2 = (f32[2048,768]{1,0:T(8,128)}, s32[1]{0:T(128)}) custom-call(s32[1]{0:T(128)} %get-tuple-element.54.q_ref, bf16[1024,1024]{1,0:T(8,128)(2,1)S(1)} %copy-done.13, bf16[1024,1024]{1,0:T(8,128)(2,1)S(1)} %collective-permute-done.9.other_ref, bf16[32,6,16,256]{3,2,1,0:T(8,128)(2,1)S(1)} %tie.4.tm_ref, ...), custom_call_target="tpu_custom_call" | custom-call | tf_op jit(solution)/shard_map/near_scores/pallas_call | solution.py:242
  119.3 5.9 %near_scores.3 = (f32[2048,768]{1,0:T(8,128)}, s32[1]{0:T(128)}) custom-call(s32[1]{0:T(128)} %get-tuple-element.57.q_ref, bf16[1024,1024]{1,0:T(8,128)(2,1)S(1)} %copy-done.12, bf16[1024,1024]{1,0:T(8,128)(2,1)S(1)} %collective-permute-done.11.other_ref, bf16[32,6,16,256]{3,2,1,0:T(8,128)(2,1)S(1)} %tie.4.tm_ref, ...), custom_call_target="tpu_custom_call", output_to_operand_aliasing={{0}: (6, {})} | custom-call | tf_op jit(solution)/shard_map/near_scores/pallas_call | solution.py:242
  125.3 1.9 %add_scores.5.old_ref = f32[2048,768]{1,0:T(8,128)} custom-call(bf16[512,256]{1,0:T(8,128)(2,1)S(1)} %copy-done.6, f32[2048,768]{1,0:T(8,128)} %get-tuple-element.62.old_ref), custom_call_target="tpu_custom_call", output_to_operand_aliasing={{}: (1, {})} | custom-call | tf_op jit(solution)/shard_map/add_scores/pallas_call | solution.py:265
  127.2 1.9 %add_scores.6.old_ref = f32[2048,768]{1,0:T(8,128)} custom-call(bf16[512,256]{1,0:T(8,128)(2,1)S(1)} %copy-done.8, f32[2048,768]{1,0:T(8,128)} %add_scores.5.old_ref), custom_call_target="tpu_custom_call", output_to_operand_aliasing={{}: (1, {})} | custom-call | tf_op jit(solution)/shard_map/add_scores/pallas_call | solution.py:265
  129.1 2.1 %add_scores.7.old_ref = f32[2048,768]{1,0:T(8,128)} custom-call(bf16[1024,256]{1,0:T(8,128)(2,1)S(1)} %collective-permute-done.5.rest_0_.got_ref, f32[2048,768]{1,0:T(8,128)} %add_scores.6.old_ref), custom_call_target="tpu_custom_call", output_to_operand_aliasing={{}: (1, {})} | custom-call | tf_op jit(solution)/shard_map/add_scores/pallas_call | solution.py:265
  131.1 2.1 %add_scores.8.old_ref = f32[2048,768]{1,0:T(8,128)} custom-call(bf16[1024,256]{1,0:T(8,128)(2,1)S(1)} %collective-permute-done.8.got_ref, f32[2048,768]{1,0:T(8,128)} %add_scores.7.old_ref), custom_call_target="tpu_custom_call", output_to_operand_aliasing={{}: (1, {})} | custom-call | tf_op jit(solution)/shard_map/add_scores/pallas_call | solution.py:265
  134.3 2.1 %add_scores.9 = f32[2048,768]{1,0:T(8,128)} custom-call(bf16[1024,256]{1,0:T(8,128)(2,1)S(1)} %collective-permute-done.7.got_ref, f32[2048,768]{1,0:T(8,128)} %add_scores.8.old_ref), custom_call_target="tpu_custom_call", output_to_operand_aliasing={{}: (1, {})} | custom-call | tf_op jit(solution)/shard_map/add_scores/pallas_call | solution.py:265
  (57 shorter events, 13.3 us)
Async XLA Ops:
  0.0 22.5 %copy-start.14 = (s32[6]{0:T(128)S(1)}, s32[6]{0:T(128)}, u32[]{:S(2)}) copy-start(s32[6]{0:T(128)} %owners_ref.1) | copy-start | bytes 76
  24.8 26.8 %all-to-all-start.1 = ((bf16[32,6,16,256]{3,2,1,0:T(8,128)(2,1)}), bf16[32,6,16,256]{3,2,1,0:T(8,128)(2,1)S(1)}, u32[]{:S(2)}, u32[]{:S(2)}) async-start(bf16[32,6,16,256]{3,2,1,0:T(8,128)(2,1)} %get-tuple-element.38), calls=%async_computation.1 | async-start | bytes 3145728 | tf_op jit(solution)/shard_map/all_to_all | solution.py:295
  49.6 4.6 %collective-permute-start = (bf16[1024,1024]{1,0:T(8,128)(2,1)}, bf16[1024,1024]{1,0:T(8,128)(2,1)}, u32[]{:S(2)}, u32[]{:S(2)}) collective-permute-start(bf16[1024,1024]{1,0:T(8,128)(2,1)} %get-tuple-element.37), channel_id=1, source_target_pairs={{0,32},{32,0},{64,96},{96,64},{1,33},{33,1},{65,97},{97,65},{2,34}... | collective-permute-start | bytes 6291464 | tf_op jit(solution)/shard_map/ppermute | solution.py:299
  51.6 4.5 %copy-start.1 = (bf16[1024,1024]{1,0:T(8,128)(2,1)S(1)}, bf16[1024,1024]{1,0:T(8,128)(2,1)}, u32[]{:S(2)}) copy-start(bf16[1024,1024]{1,0:T(8,128)(2,1)} %get-tuple-element.36.mine_ref) | copy-start | bytes 6291460
  52.3 3.7 %collective-permute-start.1 = (bf16[32,6,16,256]{3,2,1,0:T(8,128)(2,1)S(1)}, bf16[32,6,16,256]{3,2,1,0:T(8,128)(2,1)S(1)}, u32[]{:S(2)}, u32[]{:S(2)}) collective-permute-start(bf16[32,6,16,256]{3,2,1,0:T(8,128)(2,1)S(1)} %tie.4.tm_ref), channel_id=1, source_target_pairs={{0,32},{32,0},{64,96},{96,64},{1,33},{33,1},{65,97},{97,65},{2,34}... | collective-permute-start | bytes 4718600 | tf_op jit(solution)/shard_map/ppermute | solution.py:301
  59.5 5.2 %collective-permute-start.2 = (bf16[1024,1024]{1,0:T(8,128)(2,1)S(1)}, bf16[1024,1024]{1,0:T(8,128)(2,1)S(1)}, u32[]{:S(2)}, u32[]{:S(2)}) collective-permute-start(bf16[1024,1024]{1,0:T(8,128)(2,1)S(1)} %tie.5), channel_id=1, source_target_pairs={{0,32},{32,0},{64,96},{96,64},{1,33},{33,1},{65,97},{97,65},{2,34}... | collective-permute-start | bytes 6291464 | tf_op jit(solution)/shard_map/ppermute | solution.py:317
  59.7 4.9 %copy-start.2 = (bf16[1024,1024]{1,0:T(8,128)(2,1)S(1)}, bf16[1024,1024]{1,0:T(8,128)(2,1)}, u32[]{:S(2)}) copy-start(bf16[1024,1024]{1,0:T(8,128)(2,1)} %get-tuple-element.41.mine_ref) | copy-start | bytes 6291460
  59.7 9.1 %collective-permute-start.3 = (bf16[512,256]{1,0:T(8,128)(2,1)S(1)}, bf16[512,256]{1,0:T(8,128)(2,1)S(1)}, u32[]{:S(2)}, u32[]{:S(2)}) collective-permute-start(bf16[512,256]{1,0:T(8,128)(2,1)S(1)} %get-tuple-element.44), channel_id=1, source_target_pairs={{0,64},{32,96},{64,0},{96,32},{1,65},{33,97},{65,1},{97,33},{2,66}... | collective-permute-start | bytes 786440 | tf_op jit(solution)/shard_map/ppermute | solution.py:315
  63.3 11.1 %collective-permute-start.4 = (bf16[512,256]{1,0:T(8,128)(2,1)S(1)}, bf16[512,256]{1,0:T(8,128)(2,1)S(1)}, u32[]{:S(2)}, u32[]{:S(2)}) collective-permute-start(bf16[512,256]{1,0:T(8,128)(2,1)S(1)} %get-tuple-element.46), channel_id=1, source_target_pairs={{0,64},{32,96},{64,0},{96,32},{1,65},{33,97},{65,1},{97,33},{2,66}... | collective-permute-start | bytes 786440 | tf_op jit(solution)/shard_map/ppermute | solution.py:315
  64.6 9.8 %copy-start.3 = (bf16[1024,1024]{1,0:T(8,128)(2,1)}, bf16[1024,1024]{1,0:T(8,128)(2,1)S(1)}, u32[]{:S(2)}) copy-start(bf16[1024,1024]{1,0:T(8,128)(2,1)S(1)} %collective-permute-done.2.other_ref) | copy-start | bytes 6291460
  67.6 31.6 %collective-permute-start.5 = (bf16[1024,256]{1,0:T(8,128)(2,1)}, bf16[1024,256]{1,0:T(8,128)(2,1)S(1)}, u32[]{:S(2)}, u32[]{:S(2)}) collective-permute-start(bf16[1024,256]{1,0:T(8,128)(2,1)} %get-tuple-element.49), channel_id=1, source_target_pairs={{0,64},{32,96},{64,0},{96,32},{1,65},{33,97},{65,1},{97,33},{2,66}... | collective-permute-start | bytes 1572872 | tf_op jit(solution)/shard_map/ppermute | solution.py:315
  68.8 4.2 %copy-start.5 = (bf16[512,256]{1,0:T(8,128)(2,1)}, bf16[512,256]{1,0:T(8,128)(2,1)S(1)}, u32[]{:S(2)}) copy-start(bf16[512,256]{1,0:T(8,128)(2,1)S(1)} %collective-permute-done.3.rest_0_.got_ref) | copy-start | bytes 786436
  73.0 29.9 %collective-permute-start.6 = (bf16[1024,256]{1,0:T(8,128)(2,1)}, bf16[1024,256]{1,0:T(8,128)(2,1)S(1)}, u32[]{:S(2)}, u32[]{:S(2)}) collective-permute-start(bf16[1024,256]{1,0:T(8,128)(2,1)} %get-tuple-element.51), channel_id=1, source_target_pairs={{0,64},{32,96},{64,0},{96,32},{1,65},{33,97},{65,1},{97,33},{2,66}... | collective-permute-start | bytes 1572872 | tf_op jit(solution)/shard_map/ppermute | solution.py:315
  74.4 3.0 %copy-start.7 = (bf16[512,256]{1,0:T(8,128)(2,1)}, bf16[512,256]{1,0:T(8,128)(2,1)S(1)}, u32[]{:S(2)}) copy-start(bf16[512,256]{1,0:T(8,128)(2,1)S(1)} %collective-permute-done.4.rest_0_.rest_1_.got_ref) | copy-start | bytes 786436
  77.5 30.1 %collective-permute-start.10 = (bf16[1024,256]{1,0:T(8,128)(2,1)}, bf16[1024,256]{1,0:T(8,128)(2,1)S(1)}, u32[]{:S(2)}, u32[]{:S(2)}) collective-permute-start(bf16[1024,256]{1,0:T(8,128)(2,1)} %get-tuple-element.60), channel_id=1, source_target_pairs={{0,64},{32,96},{64,0},{96,32},{1,65},{33,97},{65,1},{97,33},{2,66}... | collective-permute-start | bytes 1572872 | tf_op jit(solution)/shard_map/ppermute | solution.py:315
  99.2 3.7 %copy-start.10 = (bf16[1024,1024]{1,0:T(8,128)(2,1)S(1)}, bf16[1024,1024]{1,0:T(8,128)(2,1)}, u32[]{:S(2)}) copy-start(bf16[1024,1024]{1,0:T(8,128)(2,1)} %get-tuple-element.56.refs_1_) | copy-start | bytes 6291460
  102.9 4.7 %copy-start.9 = (bf16[1024,1024]{1,0:T(8,128)(2,1)S(1)}, bf16[1024,1024]{1,0:T(8,128)(2,1)}, u32[]{:S(2)}) copy-start(bf16[1024,1024]{1,0:T(8,128)(2,1)} %get-tuple-element.59.refs_1_) | copy-start | bytes 6291460
  103.7 9.6 %collective-permute-start.9 = (bf16[1024,1024]{1,0:T(8,128)(2,1)S(1)}, bf16[1024,1024]{1,0:T(8,128)(2,1)S(1)}, u32[]{:S(2)}, u32[]{:S(2)}) collective-permute-start(bf16[1024,1024]{1,0:T(8,128)(2,1)S(1)} %tie.6), channel_id=1, source_target_pairs={{0,32},{32,0},{64,96},{96,64},{1,33},{33,1},{65,97},{97,65},{2,34}... | collective-permute-start | bytes 6291464 | tf_op jit(solution)/shard_map/ppermute | solution.py:320
  108.4 10.9 %collective-permute-start.11 = (bf16[1024,1024]{1,0:T(8,128)(2,1)S(1)}, bf16[1024,1024]{1,0:T(8,128)(2,1)S(1)}, u32[]{:S(2)}, u32[]{:S(2)}) collective-permute-start(bf16[1024,1024]{1,0:T(8,128)(2,1)S(1)} %tie.7), channel_id=1, source_target_pairs={{0,32},{32,0},{64,96},{96,64},{1,33},{33,1},{65,97},{97,65},{2,34}... | collective-permute-start | bytes 6291464 | tf_op jit(solution)/shard_map/ppermute | solution.py:320
  108.7 4.6 %copy-start.13 = (bf16[1024,1024]{1,0:T(8,128)(2,1)S(1)}, bf16[1024,1024]{1,0:T(8,128)(2,1)}, u32[]{:S(2)}) copy-start(bf16[1024,1024]{1,0:T(8,128)(2,1)} %get-tuple-element.55.mine_ref) | copy-start | bytes 6291460
  108.7 22.4 %collective-permute-start.8 = (bf16[1024,256]{1,0:T(8,128)(2,1)S(1)}, bf16[1024,256]{1,0:T(8,128)(2,1)S(1)}, u32[]{:S(2)}, u32[]{:S(2)}) collective-permute-start(bf16[1024,256]{1,0:T(8,128)(2,1)S(1)} %get-tuple-element.53), channel_id=1, source_target_pairs={{0,64},{32,96},{64,0},{96,32},{1,65},{33,97},{65,1},{97,33},{2,66}... | collective-permute-start | bytes 1572872 | tf_op jit(solution)/shard_map/ppermute | solution.py:315
  112.2 22.1 %collective-permute-start.7 = (bf16[1024,256]{1,0:T(8,128)(2,1)S(1)}, bf16[1024,256]{1,0:T(8,128)(2,1)S(1)}, u32[]{:S(2)}, u32[]{:S(2)}) collective-permute-start(bf16[1024,256]{1,0:T(8,128)(2,1)S(1)} %get-tuple-element.52), channel_id=1, source_target_pairs={{0,64},{32,96},{64,0},{96,32},{1,65},{33,97},{65,1},{97,33},{2,66}... | collective-permute-start | bytes 1572872 | tf_op jit(solution)/shard_map/ppermute | solution.py:315
  113.3 6.0 %copy-start.12 = (bf16[1024,1024]{1,0:T(8,128)(2,1)S(1)}, bf16[1024,1024]{1,0:T(8,128)(2,1)}, u32[]{:S(2)}) copy-start(bf16[1024,1024]{1,0:T(8,128)(2,1)} %get-tuple-element.58.mine_ref) | copy-start | bytes 6291460
  119.3 5.9 %copy-start.6 = (bf16[512,256]{1,0:T(8,128)(2,1)S(1)}, bf16[512,256]{1,0:T(8,128)(2,1)}, u32[]{:S(2)}) copy-start(bf16[512,256]{1,0:T(8,128)(2,1)} %copy-done.5) | copy-start | bytes 786436
  (4 other events, 8.2 us)
